TPU v7x, 256 devices: a whole 4x4x8 slice. The times are simulated.
256 devices in a mesh: dp: 2 (over x_lo), row: 16 (over z, core), col: 8 (over x_hi, y).
Axes of the slice: x: 4 (x_hi: 2, x_lo: 2; x = x_hi * 2 + x_lo), y: 4, z: 8, core: 2. Of those that a mesh axis runs over, the one named last changes fastest.
Arguments:
- grad_parts: bfloat16 [2, 2, 2048, 8, 2048], P('dp', None, 'row', None, 'col'), may hold values from -6 to 6
- out_basis: bfloat16 [2, 2048, 2048], P('dp', None, 'row'), may hold values from -0.125 to 0.125
- in_basis: bfloat16 [8, 2048, 2048], P('col'), may hold values from -0.125 to 0.125
- moments: float32 [2, 2048, 8, 2048], P('dp', 'row', 'col'), may hold values from 0.05 to 1
Outputs:
- moments_next: float32 [2, 2048, 8, 2048], P('dp', 'row', 'col')
- update: bfloat16 [2, 2048, 8, 2048], P('dp', 'row', 'col')
All inputs are finite; a program needn't handle non-finite values.
Results may differ from a plain program's by a relative error of at most 0.027.
Values may be sent and summed in bfloat16 or wider, within the bound.
No kernel may reach another device: no remote copies, remote signals or barrier semaphores. Data moves between devices by JAX's collectives and lax.ppermute only.
A program may use at most 64 MiB of HBM per device.

v0:
```python
import jax
import jax.numpy as jnp
from jax import lax
from jax.sharding import PartitionSpec as P

ema_decay = 0.9
damping = 0.1


def shards(grad_parts, out_basis, in_basis, moments):
    partials = grad_parts[0].astype(jnp.float32)
    summed = lax.psum_scatter(
        partials.astype(jnp.bfloat16), "dp", scatter_dimension=0, tiled=True
    ).astype(jnp.float32)
    gradient = summed[0].astype(jnp.bfloat16)
    gradient = lax.all_to_all(gradient, "col", split_axis=1, concat_axis=2, tiled=True)
    row_count, block_count, block_width = gradient.shape
    flat_width = block_count * block_width
    half_rotated = jnp.einsum(
        "kjc,jcd->kjd", gradient, in_basis, preferred_element_type=jnp.float32
    )
    half_rotated = half_rotated.astype(jnp.bfloat16).reshape(row_count, flat_width)
    col_panel = out_basis[0]
    moment_rows = moments[0].reshape(row_count, flat_width)
    row_panel = lax.all_to_all(col_panel, "row", split_axis=0, concat_axis=1, tiled=True)
    section = col_panel
    rotated = lax.dot_general(
        section,
        lax.all_gather(half_rotated, "row", axis=0, tiled=True),
        (((0,), (0,)), ((), ())),
        preferred_element_type=jnp.float32,
    )
    new_moments = ema_decay * moment_rows + (1.0 - ema_decay) * rotated * rotated
    scaled = (rotated / (new_moments + damping)).astype(jnp.bfloat16)
    section = row_panel
    turned_back = jnp.dot(
        section,
        lax.all_gather(scaled, "row", axis=0, tiled=True),
        preferred_element_type=jnp.float32,
    ).astype(jnp.bfloat16)
    turned_back = turned_back.reshape(row_count, block_count, block_width)
    update = jnp.einsum(
        "kjd,jcd->kjc", turned_back, in_basis, preferred_element_type=jnp.float32
    ).astype(jnp.bfloat16)
    new_moments = new_moments.reshape(1, row_count, block_count, block_width)
    return (new_moments, update.reshape(1, row_count, block_count, block_width))


def solution(mesh):
    placed = (
        P("dp", None, "row", None, "col"),
        P("dp", None, "row"),
        P("col", None, None),
        P("dp", "row", "col", None),
    )
    return jax.shard_map(
        shards,
        mesh=mesh,
        in_specs=placed,
        out_specs=(P("dp", "row", "col", None), P("dp", "row", "col", None)),
        check_vma=False,
    )
```

profile of v0, /device:TPU:1, one launch (start us, length us, event | category | flops | bytes accessed | tf_op | source)
XLA Modules:
  0.0 226.2 jit_solution(15117562645269776573)
XLA Ops:
  7.2 0.0 copy-start
  7.2 0.0 reduce-scatter.2.cloned.1.call-start
  7.2 2.5 %copy.23 = bf16[1,2,128,8,256]{4,2,3,1,0:T(8,128)(2,1)} copy(bf16[1,2,128,8,256]{4,3,2,1,0:T(8,128)(2,1)} %param.4) | data formatting | bytes 2097152 | tf_op args[0]
  9.7 0.0 copy-start.1
  9.7 0.0 reduce-scatter.2.cloned.1.call-update
  9.8 0.0 all-gather.6.cloned.1.call-start
  9.8 30.5 %reduce-scatter.2.cloned.1.call-done = bf16[1,128,8,256]{3,1,2,0:T(8,128)(2,1)} async-done(((bf16[2,128,8,256]{3,1,2,0:T(8,128)(2,1)}), bf16[1,128,8,256]{3,1,2,0:T(8,128)(2,1)}) %reduce-scatter.2.cloned.1.call-update) | async-done | bytes 524304 | tf_op jit(solution)/shard_map/reduce_scatter | solution.py:12
  40.3 16.1 %all_to_all.28 = bf16[128,8,256]{2,0,1:T(8,128)(2,1)S(1)} all-to-all(bf16[128,8,256]{2,0,1:T(8,128)(2,1)} %bitcast.64), channel_id=1, replica_groups=mesh['dp'=2,'row'=16,'col'=8] {'col'}, dimensions={1} | all-to-all | bytes 1048576 | tf_op jit(solution)/shard_map/all_to_all | solution.py:16
  56.4 0.3 copy.19
  56.7 6.6 %fusion.18 = bf16[128,1,2048]{0,2,1:T(8,128)(2,1)} fusion(bf16[128,2048]{0,1:T(8,128)(2,1)S(1)} %bitcast.65, bf16[1,2048,2048]{2,1,0:T(8,128)(2,1)} %param.6), kind=kOutput, calls=%fused_computation.11 | convolution fusion | flops 1074003968 | bytes 9437184 | tf_op jit(solution)/shard_map/kjc,jcd->kjd/dot_general | solution.py:19
  63.2 0.0 all-gather.6.cloned.1.call-update
  63.3 0.0 all-gather.4.cloned.1.call-start
  63.3 0.0 copy-done
  63.3 0.7 copy.17
  64.1 65.1 %all-gather.6.cloned.1.call-done = bf16[2048,1,2048]{0,2,1:T(8,128)(2,1)} async-done(((bf16[128,1,2048]{0,2,1:T(8,128)(2,1)}), bf16[2048,1,2048]{0,2,1:T(8,128)(2,1)}) %all-gather.6.cloned.1.call-update) | async-done | bytes 8388624 | tf_op jit(solution)/shard_map/all_gather | solution.py:29
  129.2 0.0 copy-done.1
  129.2 6.5 %divide_convert_fusion = (bf16[128,2048]{0,1:T(8,128)(2,1)}, f32[1,128,1,2048]{1,3,2,0:T(8,128)S(1)}) fusion(f32[1,128,1,2048]{1,3,2,0:T(8,128)S(1)} %copy.17, bf16[1,2048,128]{2,1,0:T(8,128)(2,1)S(1)} %copy-done.1, bf16[2048,1,2048]{0,2,1:T(8,128)(2,1)} %all-gather.6.cloned.1.call-done), kind=kOutput, calls=%fused_computation.15 | convolution fusion | flops 1075576832 | bytes 11534336 | tf_op jit(solution)/shard_map/dot_general | solution.py:27
  135.7 0.0 all-gather.4.cloned.1.call-update
  135.7 22.8 %all_to_all.29 = bf16[16,128,128]{2,1,0:T(8,128)(2,1)S(1)} all-to-all(bf16[16,128,128]{2,1,0:T(8,128)(2,1)S(1)} %bitcast.63), channel_id=1, replica_groups=mesh['dp'=2,'row'=16,'col'=8] {'row'}, dimensions={0} | all-to-all | bytes 1048576 | tf_op jit(solution)/shard_map/all_to_all | solution.py:25
  158.5 0.3 copy.20
  158.8 1.9 copy.21
  160.7 43.8 %all-gather.4.cloned.1.call-done = bf16[2048,2048]{0,1:T(8,128)(2,1)} async-done(((bf16[128,2048]{0,1:T(8,128)(2,1)}), bf16[2048,2048]{0,1:T(8,128)(2,1)}) %all-gather.4.cloned.1.call-update) | async-done | bytes 8388624 | tf_op jit(solution)/shard_map/all_gather | solution.py:38
  204.5 15.2 %fusion.15 = bf16[1,128,1,2048]{3,1,2,0:T(8,128)(2,1)} fusion(bf16[1,2048,2048]{2,1,0:T(8,128)(2,1)} %param.6, bf16[2048,2048]{0,1:T(8,128)(2,1)} %all-gather.4.cloned.1.call-done, bf16[128,2048]{0,1:T(8,128)(2,1)S(1)} %bitcast.61), kind=kOutput, calls=%fused_computation.10 | convolution fusion | flops 2148007936 | bytes 17825792 | tf_op jit(solution)/shard_map/kjd,jcd->kjc/dot_general | solution.py:42
Async XLA Ops:
  7.2 56.1 %copy-start = (f32[1,128,1,2048]{3,2,1,0:T(1,128)S(1)}, f32[1,128,1,2048]{3,2,1,0:T(1,128)}, u32[]{:S(2)}) copy-start(f32[1,128,1,2048]{3,2,1,0:T(1,128)} %param.7) | copy-start | bytes 3145732
  7.2 33.1 %reduce-scatter.2.cloned.1.call-start = ((), (), s32[]{:S(2)}) async-start(), calls=%async_computation.3 | async-start | bytes 1572864 | tf_op jit(solution)/shard_map/reduce_scatter | solution.py:12
  9.7 119.5 %copy-start.1 = (bf16[1,2048,128]{2,1,0:T(8,128)(2,1)S(1)}, bf16[1,2048,128]{2,1,0:T(8,128)(2,1)}, u32[]{:S(2)}) copy-start(bf16[1,2048,128]{2,1,0:T(8,128)(2,1)} %param.5) | copy-start | bytes 1572868
  9.8 119.4 %all-gather.6.cloned.1.call-start = ((), (), s32[]{:S(2)}) async-start(), calls=%async_computation.5 | async-start | bytes 8912896 | tf_op jit(solution)/shard_map/all_gather | solution.py:29
  63.3 141.2 %all-gather.4.cloned.1.call-start = ((), (), s32[]{:S(2)}) async-start(), calls=%async_computation.4 | async-start | bytes 8912896 | tf_op jit(solution)/shard_map/all_gather | solution.py:38
Sparse Core Ops, SparseCore 0:
  11.1 29.1 reduce-scatter.1
  63.4 65.7 all-gather.5
  135.9 68.5 all-gather.3
where the time goes:
time: 226 us
  waiting for transfers between devices  139 us (62%)
  blocking collectives  38.9 us (17%)
  matrix products  28.3 us (13%)
  between operations  13.8 us (6%)
  local copies, waits for them, and re-layouts  5.71 us (3%)
    all_gather x1, waiting for transfers between devices, shards(): lax.all_gather(half_rotated, 'row', axis=0, tiled=True)  65.1 us
    all_gather x1, waiting for transfers between devices, shards(): lax.all_gather(scaled, 'row', axis=0, tiled=True)  43.8 us
    reduce_scatter x1, waiting for transfers between devices, shards(): lax.psum_scatter(partials.astype(jnp.bfloat16), 'dp', scatter_dimension=0...  30.5 us
    all_to_all x1, blocking collectives, shards(): lax.all_to_all(col_panel, 'row', split_axis=0, concat_axis=1, tiled=True)  22.8 us
    all_to_all x1, blocking collectives, shards(): lax.all_to_all(gradient, 'col', split_axis=1, concat_axis=2, tiled=True)  16.1 us
    dot_general x1, matrix products, shards(): jnp.einsum('kjd,jcd->kjc', turned_back, in_basis, preferred_element_type=...  15.2 us
    dot_general x1, matrix products, shards(): jnp.einsum('kjc,jcd->kjd', gradient, in_basis, preferred_element_type=jnp...  6.57 us
    dot_general x1, matrix products, shards(): lax.dot_general(section, lax.all_gather(half_rotated, 'row', axis=0, tile...  6.54 us
  transfers between devices with their start and end apart: 3, of which 3 were waited for; matrix products, arithmetic and copies ran while one was open for 1% of the time, Pallas kernels for 0%

commit v1 on v0

v1 whole, which is shorter than its diff:
```python
import jax
import jax.numpy as jnp
from jax import lax
from jax.sharding import PartitionSpec as P

ema_decay = 0.9
damping = 0.1


def shards(grad_parts, out_basis, in_basis, moments):
    f32, bf16 = jnp.float32, jnp.bfloat16
    rows, blocks, width = grad_parts.shape[2:]
    count = out_basis.shape[1] // rows
    order = in_basis.shape[1]
    chunk = order // count

    basis = lax.all_gather(out_basis[0], "row", axis=0, tiled=False)
    sent = grad_parts[0].transpose(0, 2, 1, 3).reshape(-1, rows, width)
    parts = lax.all_to_all(sent, ("dp", "col"), split_axis=0, concat_axis=0, tiled=True)
    parts = parts.reshape(-1, blocks, rows, width)
    gradient = jnp.sum(parts.astype(f32), axis=0).astype(bf16)
    half = lax.dot_general(
        gradient.transpose(1, 0, 2).reshape(rows, order),
        in_basis[0],
        (((1,), (0,)), ((), ())),
        preferred_element_type=f32,
    ).astype(bf16)
    moment_rows = moments.reshape(rows, order)

    def to_columns(x):
        return x.reshape(rows, count, chunk).transpose(1, 0, 2)

    both = jnp.stack([to_columns(half), to_columns(moment_rows.astype(bf16))], axis=1)
    both = lax.all_to_all(both, "row", split_axis=0, concat_axis=0, tiled=True)
    half_cols = both[:, 0].reshape(-1, chunk)
    moment_cols = both[:, 1].astype(f32)
    rotated = jnp.einsum("pkr,kd->prd", basis, half_cols, preferred_element_type=f32)
    scaled = (
        rotated
        / (ema_decay * moment_cols + (1.0 - ema_decay) * rotated * rotated + damping)
    ).astype(bf16)
    turned = jnp.einsum("pkr,prd->kd", basis, scaled, preferred_element_type=f32)
    turned = turned.astype(bf16).reshape(count, rows, chunk)
    back = jnp.stack([turned, rotated.astype(bf16)], axis=1)
    back = lax.all_to_all(back, "row", split_axis=0, concat_axis=0, tiled=True)
    turned_rows = back[:, 0].transpose(1, 0, 2).reshape(rows, order)
    rotated_rows = back[:, 1].astype(f32).transpose(1, 0, 2).reshape(rows, order)
    update = lax.dot_general(
        turned_rows,
        in_basis[0],
        (((1,), (1,)), ((), ())),
        preferred_element_type=f32,
    ).astype(bf16)
    new_moments = ema_decay * moment_rows + (1.0 - ema_decay) * rotated_rows * rotated_rows
    return (
        new_moments.reshape(1, rows, 1, order),
        update.reshape(1, rows, 1, order),
    )


def solution(mesh):
    placed = (
        P("dp", None, "row", None, "col"),
        P("dp", None, "row"),
        P("col", None, None),
        P("dp", "row", "col", None),
    )
    return jax.shard_map(
        shards,
        mesh=mesh,
        in_specs=placed,
        out_specs=(P("dp", "row", "col", None), P("dp", "row", "col", None)),
        check_vma=False,
    )
```

time: 226 us -> 153 us (0.68)
  waiting for transfers between devices: 139 us -> 15.8 us
  blocking collectives: 38.9 us -> 83.2 us
  matrix products: 28.3 us -> 19.5 us
  starting transfers between devices: 0.12 us -> 7.62 us
  other arithmetic: 0 us -> 5.54 us
    all_gather x2 -> x1, waiting for transfers between devices: 109 us -> 3.1 us  [shards(): basis = lax.all_gather(out_basis[0], 'row', axis=0, tiled=False)]
    all_to_all x2, blocking collectives: 38.9 us -> 83.2 us  [the longest x1 50.2 us: shards(): both = lax.all_to_all(both, 'row', split_axis=0, concat_axis=0, tiled=True)]
    reduce_scatter x1 -> x0, waiting for transfers between devices: 30.5 us -> none  [shards(): lax.psum_scatter(partials.astype(jnp.bfloat16), 'dp', scatter_dimension=0...]
    all_to_all x0 -> x1, waiting for transfers between devices: none -> 12 us  [shards(): lax.all_to_all(sent, ('dp', 'col'), split_axis=0, concat_axis=0, tiled=True)]
    dot_general x3 -> x4, matrix products: 28.3 us -> 19.5 us  [the longest x1 7.12 us: shards(): lax.dot_general(turned_rows, in_basis[0], (((1,), (1,)), ((), ())), prefe...]
    all_to_all x0 -> x1, starting transfers between devices: none -> 7.58 us  [shards(): lax.all_to_all(sent, ('dp', 'col'), split_axis=0, concat_axis=0, tiled=True)]
    add x0 -> x1, other arithmetic: none -> 2.77 us  [shards(): ema_decay * moment_rows + (1.0 - ema_decay) * rotated_rows * rotated_rows]
    unnamed x7 -> x5, local copies, waits for them, and re-layouts: 5.15 us -> 3.31 us
  transfers between devices with their start and end apart: 3 -> 2, of which waited for: 3 -> 2; matrix products, arithmetic and copies ran while one was open for 1% -> 8% of each run, Pallas kernels for 0% -> 0%
where the time goes in v1:
time: 153 us
  blocking collectives  83.2 us (54%)
  matrix products  19.5 us (13%)
  waiting for transfers between devices  15.8 us (10%)
  between operations  14.2 us (9%)
  starting transfers between devices  7.62 us (5%)
  local copies, waits for them, and re-layouts  6.76 us (4%)
  other arithmetic  5.54 us (4%)
    all_to_all x1, blocking collectives, shards(): both = lax.all_to_all(both, 'row', split_axis=0, concat_axis=0, tiled=True)  50.2 us
    all_to_all x1, blocking collectives, shards(): back = lax.all_to_all(back, 'row', split_axis=0, concat_axis=0, tiled=True)  33 us
    all_to_all x1, waiting for transfers between devices, shards(): lax.all_to_all(sent, ('dp', 'col'), split_axis=0, concat_axis=0, tiled=True)  12 us
    all_to_all x1, starting transfers between devices, shards(): lax.all_to_all(sent, ('dp', 'col'), split_axis=0, concat_axis=0, tiled=True)  7.58 us
    dot_general x1, matrix products, shards(): lax.dot_general(turned_rows, in_basis[0], (((1,), (1,)), ((), ())), prefe...  7.12 us
    dot_general x1, matrix products, shards(): lax.dot_general(gradient.transpose(1, 0, 2).reshape(rows, order), in_basi...  4.79 us
    dot_general x1, matrix products, shards(): jnp.einsum('pkr,kd->prd', basis, half_cols, preferred_element_type=f32)  4.78 us
    unnamed x5, local copies, waits for them, and re-layouts  3.31 us
  transfers between devices with their start and end apart: 2, of which 2 were waited for; matrix products, arithmetic and copies ran while one was open for 8% of the time, Pallas kernels for 0%

profile of v1, /device:TPU:1, one launch (start us, length us, event | category | flops | bytes accessed | tf_op | source)
XLA Modules:
  0.0 152.6 jit_solution(17966831661816075577)
XLA Ops:
  7.2 0.0 all-gather.2.cloned.1.call-start
  7.2 0.7 all-gather.2.cloned.1.call-update
  7.9 2.4 %copy.19 = bf16[1,2,128,8,256]{4,2,3,1,0:T(8,128)(2,1)} copy(bf16[1,2,128,8,256]{4,3,2,1,0:T(8,128)(2,1)} %param.4) | data formatting | bytes 2097152 | tf_op args[0]
  10.3 7.6 %all-to-all-start = ((bf16[16,128,256]{2,1,0:T(8,128)(2,1)}), bf16[16,128,256]{2,1,0:T(8,128)(2,1)S(1)}, u32[]{:S(2)}, u32[]{:S(2)}) async-start(bf16[16,128,256]{2,1,0:T(8,128)(2,1)} %bitcast.2), calls=%async_computation | async-start | bytes 2097152 | tf_op jit(solution)/shard_map/all_to_all | solution.py:19
  17.9 1.9 %convert_element_type.36 = bf16[1,128,1,2048]{3,2,1,0:T(2,128)(2,1)S(1)} convert(f32[1,128,1,2048]{3,2,1,0:T(1,128)} %param.7) | non-fusion elementwise | flops 262144 | bytes 1572864 | tf_op jit(solution)/shard_map/convert_element_type | solution.py:33
  19.9 0.9 copy.22
  20.7 12.0 %all-to-all-done = bf16[16,128,256]{2,1,0:T(8,128)(2,1)S(1)} async-done(((bf16[16,128,256]{2,1,0:T(8,128)(2,1)}), bf16[16,128,256]{2,1,0:T(8,128)(2,1)S(1)}, u32[]{:S(2)}, u32[]{:S(2)}) %all-to-all-start) | async-done | bytes 1048608 | tf_op jit(solution)/shard_map/all_to_all | solution.py:19
  32.7 0.4 reduce_sum.12
  33.1 0.3 copy.20
  33.4 4.8 %fusion.5 = bf16[128,2048]{1,0:T(8,128)(2,1)S(1)} fusion(bf16[128,2048]{0,1:T(8,128)(2,1)S(1)} %bitcast.76, bf16[1,2048,2048]{2,1,0:T(8,128)(2,1)} %param.6), kind=kOutput, calls=%fused_computation.6 | convolution fusion | flops 1074003968 | bytes 9437184 | tf_op jit(solution)/shard_map/dot_general | solution.py:22
  38.2 0.3 copy.30
  38.4 0.1 pad_maximum_fusion
  38.6 50.2 %all_to_all.15 = bf16[16,2,128,128]{2,3,1,0:T(8,128)(2,1)S(1)} all-to-all(bf16[16,2,128,128]{2,3,1,0:T(8,128)(2,1)S(1)} %pad_maximum_fusion), channel_id=1, replica_groups=mesh['dp'=2,'row'=16,'col'=8] {'row'}, dimensions={0} | all-to-all | bytes 2097152 | tf_op jit(solution)/shard_map/all_to_all | solution.py:34
  88.8 0.3 copy.23
  89.1 0.2 reshape.70
  89.4 3.1 %all-gather.2.cloned.1.call-done = bf16[16,2048,128]{2,1,0:T(8,128)(2,1)} async-done(((bf16[1,2048,128]{2,1,0:T(8,128)(2,1)}), bf16[16,2048,128]{2,1,0:T(8,128)(2,1)}) %all-gather.2.cloned.1.call-update) | async-done | bytes 8388624 | tf_op jit(solution)/shard_map/all_gather | solution.py:17
  92.5 0.0 copy-start
  92.5 4.8 %convolution_bitcast_fusion.1 = f32[16,128,128]{1,2,0:T(8,128)S(1)} fusion(bf16[2048,128,1]{0,1,2:T(8,128)(2,1)S(1)} %reshape.70, bf16[16,2048,128]{2,1,0:T(8,128)(2,1)} %all-gather.2.cloned.1.call-done), kind=kOutput, calls=%fused_computation.12 | convolution fusion | flops 1073741824 | bytes 9961472 | tf_op jit(solution)/shard_map/pkr,kd->prd/dot_general | solution.py:37
  97.3 0.1 convert_bitcast_fusion
  97.3 0.9 copy-done
  98.2 2.8 %fusion.14 = bf16[2048,128]{0,1:T(8,128)(2,1)S(1)} fusion(bf16[16,2048,128]{2,1,0:T(8,128)(2,1)S(1)} %copy-done, f32[16,128,128]{1,2,0:T(8,128)S(1)} %convolution_bitcast_fusion.1, bf16[16,2,128,128]{2,3,1,0:T(8,128)(2,1)S(1)} %all_to_all.15), kind=kOutput, calls=%fused_computation.9 | convolution fusion | flops 1076101120 | bytes 10485760 | tf_op jit(solution)/shard_map/pkr,prd->kd/dot_general | solution.py:42
  101.0 0.3 copy.25
  101.3 0.3 copy.26
  101.6 0.1 pad_maximum_fusion.1
  101.7 0.1 copy.27
  101.8 0.0 copy-start.1
  101.8 33.0 %all_to_all.16 = bf16[16,2,128,128]{2,3,1,0:T(8,128)(2,1)S(1)} all-to-all(bf16[16,2,128,128]{2,3,1,0:T(8,128)(2,1)S(1)} %copy.27), channel_id=1, replica_groups=mesh['dp'=2,'row'=16,'col'=8] {'row'}, dimensions={0} | all-to-all | bytes 2097152 | tf_op jit(solution)/shard_map/all_to_all | solution.py:45
  134.9 0.1 fusion.26
  135.0 7.1 %fusion.11 = bf16[1,128,1,2048]{3,1,2,0:T(8,128)(2,1)} fusion(bf16[128,2048]{0,1:T(8,128)(2,1)S(1)} %bitcast.79, bf16[1,2048,2048]{2,1,0:T(8,128)(2,1)} %param.6), kind=kOutput, calls=%fused_computation.8 | convolution fusion | flops 1074003968 | bytes 9437184 | tf_op jit(solution)/shard_map/dot_general | solution.py:48
  142.1 0.8 copy.28
  142.9 0.0 copy-done.1
  142.9 2.8 %fusion.18 = f32[1,128,1,2048]{3,2,1,0:T(1,128)} fusion(f32[1,128,1,2048]{3,2,1,0:T(1,128)S(1)} %copy.28, f32[1,128,1,2048]{3,2,1,0:T(1,128)S(1)} %copy-done.1), kind=kLoop, calls=%fused_computation.16 | loop fusion | flops 1048576 | bytes 3145728 | tf_op jit(solution)/shard_map/add | solution.py:54
  (1 shorter events, 0.0 us)
Async XLA Ops:
  7.2 85.3 %all-gather.2.cloned.1.call-start = ((), (), s32[]{:S(2)}) async-start(), calls=%async_computation.3 | async-start | bytes 8912896 | tf_op jit(solution)/shard_map/all_gather | solution.py:17
  10.3 22.4 %all-to-all-start = ((bf16[16,128,256]{2,1,0:T(8,128)(2,1)}), bf16[16,128,256]{2,1,0:T(8,128)(2,1)S(1)}, u32[]{:S(2)}, u32[]{:S(2)}) async-start(bf16[16,128,256]{2,1,0:T(8,128)(2,1)} %bitcast.2), calls=%async_computation | async-start | bytes 2097152 | tf_op jit(solution)/shard_map/all_to_all | solution.py:19
  92.5 5.8 %copy-start = (bf16[16,2048,128]{2,1,0:T(8,128)(2,1)S(1)}, bf16[16,2048,128]{2,1,0:T(8,128)(2,1)}, u32[]{:S(2)}) copy-start(bf16[16,2048,128]{2,1,0:T(8,128)(2,1)} %all-gather.2.cloned.1.call-done) | copy-start | bytes 25165828
  101.8 41.1 %copy-start.1 = (f32[1,128,1,2048]{3,2,1,0:T(1,128)S(1)}, f32[1,128,1,2048]{3,2,1,0:T(1,128)}, u32[]{:S(2)}) copy-start(f32[1,128,1,2048]{3,2,1,0:T(1,128)} %param.7) | copy-start | bytes 3145732
Sparse Core Ops, SparseCore 0:
  9.8 82.5 all-gather.1

commit v2 on v1

v2 whole, which is shorter than its diff:
```python
import jax
import jax.numpy as jnp
from jax import lax
from jax.experimental import pallas as pl
from jax.experimental.pallas import tpu as pltpu
from jax.sharding import PartitionSpec as P

ema_decay = 0.9
damping = 0.1
f32, bf16 = jnp.float32, jnp.bfloat16
VMEM = pl.BlockSpec(memory_space=pltpu.VMEM)
SMEM = pl.BlockSpec(memory_space=pltpu.SMEM)
ANY = pl.BlockSpec(memory_space=pl.ANY)


def limit(mib):
    return pltpu.CompilerParams(vmem_limit_bytes=mib * 1024 * 1024)


def half_kernel(parts, basis, moment, out, pair, held, flat, total, arrive):
    blocks, rows, width = parts.shape[1:]
    wide = out.shape[3]
    copies = []
    for j in range(blocks):
        at = pl.ds(j * width, width)
        copies.append(pltpu.make_async_copy(parts.at[:, j], pair.at[:, j], arrive.at[0, j]))
        copies.append(pltpu.make_async_copy(basis.at[at], held.at[at], arrive.at[1, j]))
    copies.append(pltpu.make_async_copy(moment, flat, arrive.at[2, 0]))
    for copy in copies:
        copy.start()
    for j in range(blocks):
        copies[2 * j].wait()
        grad = (pair[0, j].astype(f32) + pair[1, j].astype(f32)).astype(bf16)
        copies[2 * j + 1].wait()
        part = jnp.dot(grad, held[j * width : (j + 1) * width], preferred_element_type=f32)
        if j == 0:
            total[...] = part
        elif j < blocks - 1:
            total[...] += part
        else:
            part = (total[...] + part).astype(bf16)
    copies[-1].wait()
    for i in range(out.shape[0]):
        out[i, 0] = part[:, i * wide : (i + 1) * wide]
        out[i, 1] = flat[:, i * wide : (i + 1) * wide].astype(bf16)


def half_rotate(parts, basis, moments, count):
    rows, order = moments.shape
    return pl.pallas_call(
        half_kernel,
        in_specs=[ANY] * 3,
        out_specs=VMEM,
        out_shape=jax.ShapeDtypeStruct((count, 2, rows, order // count), bf16),
        scratch_shapes=[
            pltpu.VMEM(parts.shape, bf16),
            pltpu.VMEM(basis.shape, bf16),
            pltpu.VMEM(moments.shape, f32),
            pltpu.VMEM(moments.shape, f32),
            pltpu.SemaphoreType.DMA((3, parts.shape[1])),
        ],
        compiler_params=limit(50),
        cost_estimate=pl.CostEstimate(
            flops=2 * rows * order * order, bytes_accessed=2 * order * order, transcendentals=0
        ),
        name="half_rotate",
    )(parts, basis, moments)


def stack_kernel(*refs):
    out = refs[-1]
    for i, ref in enumerate(refs[:-1]):
        out[i] = ref[...]


def stack(pieces):
    return pl.pallas_call(
        stack_kernel,
        in_specs=[VMEM] * len(pieces),
        out_specs=VMEM,
        out_shape=jax.ShapeDtypeStruct((len(pieces),) + pieces[0].shape, pieces[0].dtype),
        compiler_params=limit(8),
        cost_estimate=pl.CostEstimate(flops=0, bytes_accessed=1 << 25, transcendentals=0),
        name="stack",
    )(*pieces)


offsets = (0, -1, 1, -2, 2, -3, 3, 4)


def rotate_kernel(place, mine, *refs):
    sources, (out, flipped, scaled, held, arrive) = refs[:8], refs[8:]
    chip, core, first = place[0], place[1], place[2]
    starts = [lax.rem(first + i, 4) for i in (0, 3, 1, 2)]
    count, _, rows, width = out.shape
    chips, per = count // 2, count // 4
    copies = [
        [
            pltpu.make_async_copy(
                sources[i].at[pl.ds(2 * n, 2)], held.at[i, pl.ds(2 * n, 2)], arrive.at[n, i]
            )
            for i in range(8)
        ]
        for n in range(4)
    ]
    for some in copies:
        for copy in some:
            copy.start()
    for q in range(4):
        flipped[q] = mine[q * per : (q + 1) * per, 0].reshape(per * rows, width).T
    for n in range(8):
        if n % 2 == 0:
            for copy in copies[n // 2]:
                copy.wait()
        both = jnp.zeros((width, 2 * rows), f32)
        for q in range(4):
            rhs = jnp.concatenate(
                [held[4 * p + q, n].reshape(per * rows, rows) for p in range(2)], axis=1
            )
            both += jnp.dot(flipped[starts[q]], rhs, preferred_element_type=f32)
        for p in range(2):
            value = both[:, p * rows : (p + 1) * rows].T
            at = 2 * lax.rem(chip + offsets[n] + chips, chips) + (core if p == 0 else 1 - core)
            moment = mine[at, 1].astype(f32)
            out[at, 1] = value.astype(bf16)
            moment = ema_decay * moment + (1.0 - ema_decay) * value * value
            at = (2 * n + p) * rows
            scaled[at : at + rows] = (value / (moment + damping)).astype(bf16)
    for q in range(4):
        lhs = jnp.concatenate(
            [held[4 * p + q, n].reshape(per * rows, rows) for n in range(8) for p in range(2)],
            axis=1,
        )
        part = jnp.dot(lhs, scaled[...], preferred_element_type=f32)
        out[pl.ds(starts[q] * per, per), 0] = part.reshape(per, rows, width).astype(bf16)


def rotate(place, mine, sources):
    count, _, rows, width = mine.shape
    return pl.pallas_call(
        rotate_kernel,
        in_specs=[SMEM, VMEM] + [ANY] * 8,
        out_specs=VMEM,
        out_shape=jax.ShapeDtypeStruct(mine.shape, bf16),
        scratch_shapes=[
            pltpu.VMEM((4, width, count // 4 * rows), bf16),
            pltpu.VMEM((count * rows, width), bf16),
            pltpu.VMEM((8,) + sources[0].shape, bf16),
            pltpu.SemaphoreType.DMA((4, 8)),
        ],
        compiler_params=limit(24),
        cost_estimate=pl.CostEstimate(flops=1 << 32, bytes_accessed=1 << 25, transcendentals=0),
        name="rotate",
    )(place, mine, *sources)


def update_kernel(back, basis, moment, update, moment_next, turned):
    count, _, _, width = back.shape
    for i in range(count):
        at = slice(i * width, (i + 1) * width)
        turned[:, at] = back[i, 0]
        rotated = back[i, 1].astype(f32)
        moment_next[:, at] = ema_decay * moment[:, at] + (1.0 - ema_decay) * rotated * rotated
    step = 256
    for i in range(0, basis.shape[0], step):
        update[:, i : i + step] = lax.dot_general(
            turned[...], basis[i : i + step], (((1,), (1,)), ((), ())), preferred_element_type=f32
        ).astype(bf16)


def finish(back, basis, moments):
    rows, order = moments.shape
    return pl.pallas_call(
        update_kernel,
        in_specs=[VMEM] * 3,
        out_specs=[VMEM] * 2,
        out_shape=[
            jax.ShapeDtypeStruct((rows, order), bf16),
            jax.ShapeDtypeStruct((rows, order), f32),
        ],
        scratch_shapes=[pltpu.VMEM((rows, order), bf16)],
        compiler_params=limit(16),
        name="finish",
    )(back, basis, moments)


def shards(grad_parts, out_basis, in_basis, moments):
    rows, blocks, width = grad_parts.shape[2:]
    order = in_basis.shape[1]
    row, col = lax.axis_index("row"), lax.axis_index("col")
    count = lax.axis_size("row")
    chips = count // 2
    up = [(i, (i + 2) % count) for i in range(count)]
    down = [(b, a) for a, b in up]
    swap = [(i, i ^ 1) for i in range(count)]
    y_next = [(4 * h + y, 4 * h + (y + 1) % 4) for h in range(2) for y in range(4)]
    y_last = [(b, a) for a, b in y_next]
    x_swap = [(i, (i + 4) % 8) for i in range(8)]
    quarter = (col + 2 * (col >> 2)) & 3
    place = jnp.stack([row >> 1, row & 1, quarter]).astype(jnp.int32)

    own = lax.dynamic_slice_in_dim(out_basis[0], quarter * (order // 4), order // 4, 0)
    own = own.reshape(chips // 4, 2, rows, rows)
    a, b = lax.ppermute(own, "row", up), lax.ppermute(own, "row", down)

    sent = grad_parts[0].transpose(0, 2, 1, 3).reshape(-1, rows, width)
    parts = lax.all_to_all(sent, ("dp", "col"), split_axis=0, concat_axis=0, tiled=True)
    parts = parts.reshape(2, blocks, rows, width)

    near = [own, a, b]
    flat = moments.reshape(rows, order)
    a, b, flat = lax.optimization_barrier((a, b, flat))
    for _ in range(2):
        a, b = lax.ppermute(a, "row", up), lax.ppermute(b, "row", down)
        near += [a, b]
    near.append(lax.ppermute(a, "row", up))
    half = half_rotate(parts, in_basis[0], flat, count)
    half, near = lax.optimization_barrier((half, near))
    held = stack(near)
    quarters = [held]
    for pairs in (y_next, y_last, x_swap):
        quarters.append(lax.ppermute(held, "col", pairs))
    quarters += [lax.ppermute(x, "row", swap) for x in quarters]
    half = lax.all_to_all(half, "row", split_axis=0, concat_axis=0, tiled=True)
    back = rotate(place, half, quarters)
    back = lax.all_to_all(back, "row", split_axis=0, concat_axis=0, tiled=True)
    update, new_moments = finish(back, in_basis[0], flat)
    return new_moments.reshape(1, rows, 1, order), update.reshape(1, rows, 1, order)


def solution(mesh):
    placed = (
        P("dp", None, "row", None, "col"),
        P("dp", None, "row"),
        P("col", None, None),
        P("dp", "row", "col", None),
    )
    return jax.shard_map(
        shards,
        mesh=mesh,
        in_specs=placed,
        out_specs=(P("dp", "row", "col", None), P("dp", "row", "col", None)),
        check_vma=False,
    )
```

time: 153 us -> 131 us (0.86)
  blocking collectives: 83.2 us -> 31.9 us
  starting transfers between devices: 7.62 us -> 46.2 us
  matrix products: 19.5 us -> 0 us
  Pallas kernels: 0 us -> 16.4 us
  between operations: 14.2 us -> 0.73 us
  waiting for transfers between devices: 15.8 us -> 25.8 us
  other arithmetic: 5.54 us -> 0.08 us
  local copies, waits for them, and re-layouts: 6.76 us -> 9.51 us
    all_to_all x1 -> x0, blocking collectives: 50.2 us -> none  [shards(): both = lax.all_to_all(both, 'row', split_axis=0, concat_axis=0, tiled=True)]
    ppermute x0 -> x14, starting transfers between devices: none -> 28.2 us  [the longest x4 11.8 us: shards(): quarters += [lax.ppermute(x, 'row', swap) for x in quarters]]
    dot_general x4 -> x0, matrix products: 19.5 us -> none  [the longest x1 7.12 us: shards(): lax.dot_general(turned_rows, in_basis[0], (((1,), (1,)), ((), ())), prefe...]
    pallas_call x0 -> x4, Pallas kernels: none -> 16.4 us  [the longest x1 7.31 us: rotate(): pl.pallas_call(rotate_kernel, in_specs=[SMEM, VMEM] + [ANY] * 8, out_spec...]
    ppermute x0 -> x14, waiting for transfers between devices: none -> 14.3 us  [the longest x4 5 us: shards(): a, b = (lax.ppermute(a, 'row', up), lax.ppermute(b, 'row', down))]
    all_to_all x1, waiting for transfers between devices: 12 us -> 0.01 us  [shards(): lax.all_to_all(sent, ('dp', 'col'), split_axis=0, concat_axis=0, tiled=True)]
    all_to_all x0 -> x1, waiting for transfers between devices: none -> 11.6 us  [shards(): half = lax.all_to_all(half, 'row', split_axis=0, concat_axis=0, tiled=True)]
    all_to_all x0 -> x1, starting transfers between devices: none -> 10.4 us  [shards(): half = lax.all_to_all(half, 'row', split_axis=0, concat_axis=0, tiled=True)]
  transfers between devices with their start and end apart: 2 -> 16, of which waited for: 2 -> 7; matrix products, arithmetic and copies ran while one was open for 8% -> 1% of each run, Pallas kernels for 0% -> 3%
where the time goes in v2:
time: 131 us
  starting transfers between devices  46.2 us (35%)
  blocking collectives  31.9 us (24%)
  waiting for transfers between devices  25.8 us (20%)
  Pallas kernels  16.4 us (13%)
  local copies, waits for them, and re-layouts  9.51 us (7%)
    all_to_all x1, blocking collectives, shards(): back = lax.all_to_all(back, 'row', split_axis=0, concat_axis=0, tiled=True)  31.9 us
    ppermute x4, starting transfers between devices, shards(): quarters += [lax.ppermute(x, 'row', swap) for x in quarters]  11.8 us
    all_to_all x1, waiting for transfers between devices, shards(): half = lax.all_to_all(half, 'row', split_axis=0, concat_axis=0, tiled=True)  11.6 us
    all_to_all x1, starting transfers between devices, shards(): half = lax.all_to_all(half, 'row', split_axis=0, concat_axis=0, tiled=True)  10.4 us
    unnamed x9, local copies, waits for them, and re-layouts  9.49 us
    all_to_all x1, starting transfers between devices, shards(): lax.all_to_all(sent, ('dp', 'col'), split_axis=0, concat_axis=0, tiled=True)  7.58 us
    pallas_call x1, Pallas kernels, rotate(): pl.pallas_call(rotate_kernel, in_specs=[SMEM, VMEM] + [ANY] * 8, out_spec...  7.31 us
    ppermute x2, starting transfers between devices, shards(): a, b = (lax.ppermute(own, 'row', up), lax.ppermute(own, 'row', down))  5.66 us
  transfers between devices with their start and end apart: 16, of which 7 were waited for; matrix products, arithmetic and copies ran while one was open for 1% of the time, Pallas kernels for 3%

profile of v2, /device:TPU:1, one launch (start us, length us, event | category | flops | bytes accessed | tf_op | source)
XLA Modules:
  0.0 130.7 jit_solution(17501682551447838662)
XLA Ops:
  0.6 0.0 copy-start
  0.6 2.5 %copy.7 = bf16[1,2,128,8,256]{4,2,3,1,0:T(8,128)(2,1)} copy(bf16[1,2,128,8,256]{4,3,2,1,0:T(8,128)(2,1)} %param.4) | data formatting | bytes 2097152 | tf_op args[0]
  3.1 7.6 %all-to-all-start = ((bf16[16,128,256]{2,1,0:T(8,128)(2,1)}), bf16[16,128,256]{2,1,0:T(8,128)(2,1)S(1)}, u32[]{:S(2)}, u32[]{:S(2)}) async-start(bf16[16,128,256]{2,1,0:T(8,128)(2,1)} %bitcast.5), calls=%async_computation | async-start | bytes 2097152 | tf_op jit(solution)/shard_map/all_to_all | solution.py:207
  10.8 5.7 %collective-permute-start.1 = (bf16[2,2,128,128]{3,2,1,0:T(8,128)(2,1)S(1)}, bf16[2,2,128,128]{3,2,1,0:T(8,128)(2,1)S(1)}, u32[]{:S(2)}, u32[]{:S(2)}) collective-permute-start(bf16[2,2,128,128]{3,2,1,0:T(8,128)(2,1)S(1)} %bitcast.22), channel_id=1, source_target_pairs={{16,0},{24,8},{32,16},{40,24},{48,32},{56,40},{64,48},{72,56},{80,... | collective-permute-start | bytes 393224 | tf_op jit(solution)/shard_map/ppermute | solution.py:204
  16.4 0.0 collective-permute-start
  16.4 1.6 %copy.11 = f32[1,128,1,2048]{3,1,2,0:T(8,128)S(1)} copy(f32[1,128,1,2048]{3,2,1,0:T(1,128)} %param.7) | data formatting | bytes 2097152
  18.0 0.4 collective-permute-done.1.refs_2_
  18.4 3.4 %collective-permute-done.refs_1_ = bf16[2,2,128,128]{3,2,1,0:T(8,128)(2,1)S(1)} collective-permute-done((bf16[2,2,128,128]{3,2,1,0:T(8,128)(2,1)S(1)}, bf16[2,2,128,128]{3,2,1,0:T(8,128)(2,1)S(1)}, u32[]{:S(2)}, u32[]{:S(2)}) %collective-permute-start) | collective-permute-done | bytes 131104 | tf_op jit(solution)/shard_map/ppermute | solution.py:204
  21.7 0.0 collective-permute-start.2
  21.7 2.7 %collective-permute-start.3 = (bf16[2,2,128,128]{3,2,1,0:T(8,128)(2,1)S(1)}, bf16[2,2,128,128]{3,2,1,0:T(8,128)(2,1)S(1)}, u32[]{:S(2)}, u32[]{:S(2)}) collective-permute-start(bf16[2,2,128,128]{3,2,1,0:T(8,128)(2,1)S(1)} %collective-permute-done.1.refs_2_), channel_id=1, source_target_pairs={{16,0},{24,8},{32,16},{40,24},{48,32},{56,40},{64,48},{72,56},{80,... | collective-permute-start | bytes 393224 | tf_op jit(solution)/shard_map/ppermute | solution.py:214
  24.4 2.6 %collective-permute-done.2.refs_3_ = bf16[2,2,128,128]{3,2,1,0:T(8,128)(2,1)S(1)} collective-permute-done((bf16[2,2,128,128]{3,2,1,0:T(8,128)(2,1)S(1)}, bf16[2,2,128,128]{3,2,1,0:T(8,128)(2,1)S(1)}, u32[]{:S(2)}, u32[]{:S(2)}) %collective-permute-start.2) | collective-permute-done | bytes 131104 | tf_op jit(solution)/shard_map/ppermute | solution.py:214
  27.1 2.7 %collective-permute-start.5 = (bf16[2,2,128,128]{3,2,1,0:T(8,128)(2,1)S(1)}, bf16[2,2,128,128]{3,2,1,0:T(8,128)(2,1)S(1)}, u32[]{:S(2)}, u32[]{:S(2)}) collective-permute-start(bf16[2,2,128,128]{3,2,1,0:T(8,128)(2,1)S(1)} %collective-permute-done.3.refs_4_), channel_id=1, source_target_pairs={{16,0},{24,8},{32,16},{40,24},{48,32},{56,40},{64,48},{72,56},{80,... | collective-permute-start | bytes 393224 | tf_op jit(solution)/shard_map/ppermute | solution.py:214
  29.7 2.3 %collective-permute-done.4.refs_5_ = bf16[2,2,128,128]{3,2,1,0:T(8,128)(2,1)S(1)} collective-permute-done((bf16[2,2,128,128]{3,2,1,0:T(8,128)(2,1)S(1)}, bf16[2,2,128,128]{3,2,1,0:T(8,128)(2,1)S(1)}, u32[]{:S(2)}, u32[]{:S(2)}) %collective-permute-start.4) | collective-permute-done | bytes 131104 | tf_op jit(solution)/shard_map/ppermute | solution.py:214
  32.1 4.2 %half_rotate.1 = bf16[16,2,128,128]{3,2,1,0:T(8,128)(2,1)S(1)} custom-call(bf16[2,8,128,256]{3,2,1,0:T(8,128)(2,1)S(1)} %bitcast.20, bf16[2048,2048]{1,0:T(8,128)(2,1)} %bitcast.16, f32[128,2048]{1,0:T(8,128)S(1)} %bitcast.18), custom_call_target="tpu_custom_call" | custom-call | flops 1073741824 | bytes 8388608 | tf_op jit(solution)/shard_map/half_rotate/pallas_call | solution.py:50
  36.4 0.0 copy-start.2
  36.4 0.9 collective-permute-done.6.refs_7_
  37.2 1.0 stack.17.refs_0_
  38.2 3.0 %collective-permute-start.9 = (bf16[8,2,2,128,128]{4,3,2,1,0:T(8,128)(2,1)S(1)}, bf16[8,2,2,128,128]{4,3,2,1,0:T(8,128)(2,1)}, u32[]{:S(2)}, u32[]{:S(2)}) collective-permute-start(bf16[8,2,2,128,128]{4,3,2,1,0:T(8,128)(2,1)S(1)} %stack.17.refs_0_), channel_id=1, source_target_pairs={{0,4},{1,5},{2,6},{3,7},{4,0},{5,1},{6,2},{7,3},{8,12},{9,13},{10,... | collective-permute-start | bytes 3145736 | tf_op jit(solution)/shard_map/ppermute | solution.py:222
  41.2 2.4 %collective-permute-start.8 = (bf16[8,2,2,128,128]{4,3,2,1,0:T(8,128)(2,1)S(1)}, bf16[8,2,2,128,128]{4,3,2,1,0:T(8,128)(2,1)}, u32[]{:S(2)}, u32[]{:S(2)}) collective-permute-start(bf16[8,2,2,128,128]{4,3,2,1,0:T(8,128)(2,1)S(1)} %stack.17.refs_0_), channel_id=1, source_target_pairs={{1,0},{2,1},{3,2},{0,3},{5,4},{6,5},{7,6},{4,7},{9,8},{10,9},{11,1... | collective-permute-start | bytes 3145736 | tf_op jit(solution)/shard_map/ppermute | solution.py:222
  43.6 10.4 %all-to-all-start.1 = ((bf16[16,2,128,128]{3,2,1,0:T(8,128)(2,1)}), bf16[16,2,128,128]{3,2,1,0:T(8,128)(2,1)}, u32[]{:S(2)}, u32[]{:S(2)}) async-start(bf16[16,2,128,128]{3,2,1,0:T(8,128)(2,1)} %copy-done.2), calls=%async_computation.1 | async-start | bytes 2097152 | tf_op jit(solution)/shard_map/all_to_all | solution.py:224
  54.1 0.4 collective-permute-start.10
  54.4 4.6 %collective-permute-done.9.refs_3_ = bf16[8,2,2,128,128]{4,3,2,1,0:T(8,128)(2,1)} collective-permute-done((bf16[8,2,2,128,128]{4,3,2,1,0:T(8,128)(2,1)S(1)}, bf16[8,2,2,128,128]{4,3,2,1,0:T(8,128)(2,1)}, u32[]{:S(2)}, u32[]{:S(2)}) %collective-permute-start.9) | collective-permute-done | bytes 1048608 | tf_op jit(solution)/shard_map/ppermute | solution.py:222
  59.1 6.4 %collective-permute-start.13 = (bf16[8,2,2,128,128]{4,3,2,1,0:T(8,128)(2,1)}, bf16[8,2,2,128,128]{4,3,2,1,0:T(8,128)(2,1)}, u32[]{:S(2)}, u32[]{:S(2)}) collective-permute-start(bf16[8,2,2,128,128]{4,3,2,1,0:T(8,128)(2,1)} %collective-permute-done.9.refs_3_), channel_id=1, source_target_pairs={{0,8},{8,0},{16,24},{24,16},{32,40},{40,32},{48,56},{56,48},{64,72... | collective-permute-start | bytes 3145736 | tf_op jit(solution)/shard_map/ppermute | solution.py:223
  65.5 1.5 %collective-permute-start.12 = (bf16[8,2,2,128,128]{4,3,2,1,0:T(8,128)(2,1)}, bf16[8,2,2,128,128]{4,3,2,1,0:T(8,128)(2,1)}, u32[]{:S(2)}, u32[]{:S(2)}) collective-permute-start(bf16[8,2,2,128,128]{4,3,2,1,0:T(8,128)(2,1)} %collective-permute-done.8.refs_2_), channel_id=1, source_target_pairs={{0,8},{8,0},{16,24},{24,16},{32,40},{40,32},{48,56},{56,48},{64,72... | collective-permute-start | bytes 3145736 | tf_op jit(solution)/shard_map/ppermute | solution.py:223
  67.0 3.5 %collective-permute-start.11 = (bf16[8,2,2,128,128]{4,3,2,1,0:T(8,128)(2,1)}, bf16[8,2,2,128,128]{4,3,2,1,0:T(8,128)(2,1)}, u32[]{:S(2)}, u32[]{:S(2)}) collective-permute-start(bf16[8,2,2,128,128]{4,3,2,1,0:T(8,128)(2,1)} %collective-permute-done.7.refs_1_), channel_id=1, source_target_pairs={{0,8},{8,0},{16,24},{24,16},{32,40},{40,32},{48,56},{56,48},{64,72... | collective-permute-start | bytes 3145736 | tf_op jit(solution)/shard_map/ppermute | solution.py:223
  70.5 0.1 pad_add_fusion.place
  70.6 11.6 %all-to-all-done.1.mine = bf16[16,2,128,128]{3,2,1,0:T(8,128)(2,1)} async-done(((bf16[16,2,128,128]{3,2,1,0:T(8,128)(2,1)}), bf16[16,2,128,128]{3,2,1,0:T(8,128)(2,1)}, u32[]{:S(2)}, u32[]{:S(2)}) %all-to-all-start.1) | async-done | bytes 1048608 | tf_op jit(solution)/shard_map/all_to_all | solution.py:224
  82.1 7.3 %rotate.1 = bf16[16,2,128,128]{3,2,1,0:T(8,128)(2,1)S(1)} custom-call(s32[3]{0:T(128)S(1)} %pad_add_fusion.place, bf16[16,2,128,128]{3,2,1,0:T(8,128)(2,1)} %all-to-all-done.1.mine, bf16[8,2,2,128,128]{4,3,2,1,0:T(8,128)(2,1)S(1)} %stack.17.refs_0_, bf16[8,2,2,128,128]{4,3,2,1,0:T(8,128)(2,1)} %collective-permute-done.7.refs_1_, ...), custom_call_target="tpu_custom_call" | custom-call | flops 4294967296 | bytes 33554432 | tf_op jit(solution)/shard_map/rotate/pallas_call | solution.py:140
  89.5 31.9 %all_to_all.15.back = bf16[16,2,128,128]{3,2,1,0:T(8,128)(2,1)S(1)} all-to-all(bf16[16,2,128,128]{3,2,1,0:T(8,128)(2,1)S(1)} %rotate.1), channel_id=1, replica_groups=mesh['dp'=2,'row'=16,'col'=8] {'row'}, dimensions={0} | all-to-all | bytes 2097152 | tf_op jit(solution)/shard_map/all_to_all | solution.py:226
  121.3 3.4 %copy-done.1 = bf16[1,2048,2048]{2,1,0:T(8,128)(2,1)S(1)} copy-done((bf16[1,2048,2048]{2,1,0:T(8,128)(2,1)S(1)}, bf16[1,2048,2048]{2,1,0:T(8,128)(2,1)}, u32[]{:S(2)}) %copy-start.1) | copy-done | bytes 8388632
  124.7 3.9 %finish.1 = (bf16[128,2048]{1,0:T(8,128)(2,1)}, f32[128,2048]{1,0:T(8,128)S(1)}) custom-call(bf16[16,2,128,128]{3,2,1,0:T(8,128)(2,1)S(1)} %all_to_all.15.back, bf16[2048,2048]{1,0:T(8,128)(2,1)S(1)} %bitcast.17, f32[128,2048]{1,0:T(8,128)S(1)} %bitcast.19), custom_call_target="tpu_custom_call" | custom-call | tf_op jit(solution)/shard_map/finish/pallas_call | solution.py:173
  128.6 2.0 %copy.8 = f32[1,128,1,2048]{3,2,1,0:T(1,128)} copy(f32[1,128,1,2048]{3,1,2,0:T(8,128)S(1)} %bitcast.21) | data formatting | bytes 2097152
  (16 shorter events, 0.1 us)
Async XLA Ops:
  0.6 10.1 %copy-start = (bf16[1,2048,128]{2,1,0:T(8,128)(2,1)S(1)}, bf16[1,2048,128]{2,1,0:T(8,128)(2,1)}, u32[]{:S(2)}) copy-start(bf16[1,2048,128]{2,1,0:T(8,128)(2,1)} %param.5) | copy-start | bytes 1572868
  3.1 29.0 %all-to-all-start = ((bf16[16,128,256]{2,1,0:T(8,128)(2,1)}), bf16[16,128,256]{2,1,0:T(8,128)(2,1)S(1)}, u32[]{:S(2)}, u32[]{:S(2)}) async-start(bf16[16,128,256]{2,1,0:T(8,128)(2,1)} %bitcast.5), calls=%async_computation | async-start | bytes 2097152 | tf_op jit(solution)/shard_map/all_to_all | solution.py:207
  10.8 7.6 %collective-permute-start.1 = (bf16[2,2,128,128]{3,2,1,0:T(8,128)(2,1)S(1)}, bf16[2,2,128,128]{3,2,1,0:T(8,128)(2,1)S(1)}, u32[]{:S(2)}, u32[]{:S(2)}) collective-permute-start(bf16[2,2,128,128]{3,2,1,0:T(8,128)(2,1)S(1)} %bitcast.22), channel_id=1, source_target_pairs={{16,0},{24,8},{32,16},{40,24},{48,32},{56,40},{64,48},{72,56},{80,... | collective-permute-start | bytes 393224 | tf_op jit(solution)/shard_map/ppermute | solution.py:204
  16.4 5.3 %collective-permute-start = (bf16[2,2,128,128]{3,2,1,0:T(8,128)(2,1)S(1)}, bf16[2,2,128,128]{3,2,1,0:T(8,128)(2,1)S(1)}, u32[]{:S(2)}, u32[]{:S(2)}) collective-permute-start(bf16[2,2,128,128]{3,2,1,0:T(8,128)(2,1)S(1)} %bitcast.23), channel_id=1, source_target_pairs={{0,16},{8,24},{16,32},{24,40},{32,48},{40,56},{48,64},{56,72},{64,... | collective-permute-start | bytes 393224 | tf_op jit(solution)/shard_map/ppermute | solution.py:204
  21.7 5.3 %collective-permute-start.2 = (bf16[2,2,128,128]{3,2,1,0:T(8,128)(2,1)S(1)}, bf16[2,2,128,128]{3,2,1,0:T(8,128)(2,1)S(1)}, u32[]{:S(2)}, u32[]{:S(2)}) collective-permute-start(bf16[2,2,128,128]{3,2,1,0:T(8,128)(2,1)S(1)} %collective-permute-done.refs_1_), channel_id=1, source_target_pairs={{0,16},{8,24},{16,32},{24,40},{32,48},{40,56},{48,64},{56,72},{64,... | collective-permute-start | bytes 393224 | tf_op jit(solution)/shard_map/ppermute | solution.py:214
  21.7 5.3 %collective-permute-start.3 = (bf16[2,2,128,128]{3,2,1,0:T(8,128)(2,1)S(1)}, bf16[2,2,128,128]{3,2,1,0:T(8,128)(2,1)S(1)}, u32[]{:S(2)}, u32[]{:S(2)}) collective-permute-start(bf16[2,2,128,128]{3,2,1,0:T(8,128)(2,1)S(1)} %collective-permute-done.1.refs_2_), channel_id=1, source_target_pairs={{16,0},{24,8},{32,16},{40,24},{48,32},{56,40},{64,48},{72,56},{80,... | collective-permute-start | bytes 393224 | tf_op jit(solution)/shard_map/ppermute | solution.py:214
  27.1 5.0 %collective-permute-start.4 = (bf16[2,2,128,128]{3,2,1,0:T(8,128)(2,1)S(1)}, bf16[2,2,128,128]{3,2,1,0:T(8,128)(2,1)S(1)}, u32[]{:S(2)}, u32[]{:S(2)}) collective-permute-start(bf16[2,2,128,128]{3,2,1,0:T(8,128)(2,1)S(1)} %collective-permute-done.2.refs_3_), channel_id=1, source_target_pairs={{0,16},{8,24},{16,32},{24,40},{32,48},{40,56},{48,64},{56,72},{64,... | collective-permute-start | bytes 393224 | tf_op jit(solution)/shard_map/ppermute | solution.py:214
  27.1 9.3 %collective-permute-start.5 = (bf16[2,2,128,128]{3,2,1,0:T(8,128)(2,1)S(1)}, bf16[2,2,128,128]{3,2,1,0:T(8,128)(2,1)S(1)}, u32[]{:S(2)}, u32[]{:S(2)}) collective-permute-start(bf16[2,2,128,128]{3,2,1,0:T(8,128)(2,1)S(1)} %collective-permute-done.3.refs_4_), channel_id=1, source_target_pairs={{16,0},{24,8},{32,16},{40,24},{48,32},{56,40},{64,48},{72,56},{80,... | collective-permute-start | bytes 393224 | tf_op jit(solution)/shard_map/ppermute | solution.py:214
  32.1 5.1 %collective-permute-start.6 = (bf16[2,2,128,128]{3,2,1,0:T(8,128)(2,1)S(1)}, bf16[2,2,128,128]{3,2,1,0:T(8,128)(2,1)}, u32[]{:S(2)}, u32[]{:S(2)}) collective-permute-start(bf16[2,2,128,128]{3,2,1,0:T(8,128)(2,1)S(1)} %collective-permute-done.4.refs_5_), channel_id=1, source_target_pairs={{0,16},{8,24},{16,32},{24,40},{32,48},{40,56},{48,64},{56,72},{64,... | collective-permute-start | bytes 393224 | tf_op jit(solution)/shard_map/ppermute | solution.py:216
  36.4 7.3 %copy-start.2 = (bf16[16,2,128,128]{3,2,1,0:T(8,128)(2,1)}, bf16[16,2,128,128]{3,2,1,0:T(8,128)(2,1)S(1)}, u32[]{:S(2)}) copy-start(bf16[16,2,128,128]{3,2,1,0:T(8,128)(2,1)S(1)} %half_rotate.1) | copy-start | bytes 3145732
  38.2 20.9 %collective-permute-start.9 = (bf16[8,2,2,128,128]{4,3,2,1,0:T(8,128)(2,1)S(1)}, bf16[8,2,2,128,128]{4,3,2,1,0:T(8,128)(2,1)}, u32[]{:S(2)}, u32[]{:S(2)}) collective-permute-start(bf16[8,2,2,128,128]{4,3,2,1,0:T(8,128)(2,1)S(1)} %stack.17.refs_0_), channel_id=1, source_target_pairs={{0,4},{1,5},{2,6},{3,7},{4,0},{5,1},{6,2},{7,3},{8,12},{9,13},{10,... | collective-permute-start | bytes 3145736 | tf_op jit(solution)/shard_map/ppermute | solution.py:222
  41.2 24.3 %collective-permute-start.8 = (bf16[8,2,2,128,128]{4,3,2,1,0:T(8,128)(2,1)S(1)}, bf16[8,2,2,128,128]{4,3,2,1,0:T(8,128)(2,1)}, u32[]{:S(2)}, u32[]{:S(2)}) collective-permute-start(bf16[8,2,2,128,128]{4,3,2,1,0:T(8,128)(2,1)S(1)} %stack.17.refs_0_), channel_id=1, source_target_pairs={{1,0},{2,1},{3,2},{0,3},{5,4},{6,5},{7,6},{4,7},{9,8},{10,9},{11,1... | collective-permute-start | bytes 3145736 | tf_op jit(solution)/shard_map/ppermute | solution.py:222
  43.6 23.4 %collective-permute-start.7 = (bf16[8,2,2,128,128]{4,3,2,1,0:T(8,128)(2,1)S(1)}, bf16[8,2,2,128,128]{4,3,2,1,0:T(8,128)(2,1)}, u32[]{:S(2)}, u32[]{:S(2)}) collective-permute-start(bf16[8,2,2,128,128]{4,3,2,1,0:T(8,128)(2,1)S(1)} %stack.17.refs_0_), channel_id=1, source_target_pairs={{0,1},{1,2},{2,3},{3,0},{4,5},{5,6},{6,7},{7,4},{8,9},{9,10},{10,1... | collective-permute-start | bytes 3145736 | tf_op jit(solution)/shard_map/ppermute | solution.py:222
  43.6 38.5 %all-to-all-start.1 = ((bf16[16,2,128,128]{3,2,1,0:T(8,128)(2,1)}), bf16[16,2,128,128]{3,2,1,0:T(8,128)(2,1)}, u32[]{:S(2)}, u32[]{:S(2)}) async-start(bf16[16,2,128,128]{3,2,1,0:T(8,128)(2,1)} %copy-done.2), calls=%async_computation.1 | async-start | bytes 2097152 | tf_op jit(solution)/shard_map/all_to_all | solution.py:224
  54.1 16.5 %collective-permute-start.10 = (bf16[8,2,2,128,128]{4,3,2,1,0:T(8,128)(2,1)S(1)}, bf16[8,2,2,128,128]{4,3,2,1,0:T(8,128)(2,1)}, u32[]{:S(2)}, u32[]{:S(2)}) collective-permute-start(bf16[8,2,2,128,128]{4,3,2,1,0:T(8,128)(2,1)S(1)} %stack.17.refs_0_), channel_id=1, source_target_pairs={{0,8},{8,0},{16,24},{24,16},{32,40},{40,32},{48,56},{56,48},{64,72... | collective-permute-start | bytes 3145736 | tf_op jit(solution)/shard_map/ppermute | solution.py:223
  59.1 23.1 %collective-permute-start.13 = (bf16[8,2,2,128,128]{4,3,2,1,0:T(8,128)(2,1)}, bf16[8,2,2,128,128]{4,3,2,1,0:T(8,128)(2,1)}, u32[]{:S(2)}, u32[]{:S(2)}) collective-permute-start(bf16[8,2,2,128,128]{4,3,2,1,0:T(8,128)(2,1)} %collective-permute-done.9.refs_3_), channel_id=1, source_target_pairs={{0,8},{8,0},{16,24},{24,16},{32,40},{40,32},{48,56},{56,48},{64,72... | collective-permute-start | bytes 3145736 | tf_op jit(solution)/shard_map/ppermute | solution.py:223
  65.5 16.7 %collective-permute-start.12 = (bf16[8,2,2,128,128]{4,3,2,1,0:T(8,128)(2,1)}, bf16[8,2,2,128,128]{4,3,2,1,0:T(8,128)(2,1)}, u32[]{:S(2)}, u32[]{:S(2)}) collective-permute-start(bf16[8,2,2,128,128]{4,3,2,1,0:T(8,128)(2,1)} %collective-permute-done.8.refs_2_), channel_id=1, source_target_pairs={{0,8},{8,0},{16,24},{24,16},{32,40},{40,32},{48,56},{56,48},{64,72... | collective-permute-start | bytes 3145736 | tf_op jit(solution)/shard_map/ppermute | solution.py:223
  67.0 15.2 %collective-permute-start.11 = (bf16[8,2,2,128,128]{4,3,2,1,0:T(8,128)(2,1)}, bf16[8,2,2,128,128]{4,3,2,1,0:T(8,128)(2,1)}, u32[]{:S(2)}, u32[]{:S(2)}) collective-permute-start(bf16[8,2,2,128,128]{4,3,2,1,0:T(8,128)(2,1)} %collective-permute-done.7.refs_1_), channel_id=1, source_target_pairs={{0,8},{8,0},{16,24},{24,16},{32,40},{40,32},{48,56},{56,48},{64,72... | collective-permute-start | bytes 3145736 | tf_op jit(solution)/shard_map/ppermute | solution.py:223
  121.3 3.4 %copy-start.1 = (bf16[1,2048,2048]{2,1,0:T(8,128)(2,1)S(1)}, bf16[1,2048,2048]{2,1,0:T(8,128)(2,1)}, u32[]{:S(2)}) copy-start(bf16[1,2048,2048]{2,1,0:T(8,128)(2,1)} %param.6) | copy-start | bytes 25165828

commit v3 on v2

--- a/solution.py
+++ b/solution.py
@@ -154,31 +154,58 @@
     )(place, mine, *sources)
 
 
-def update_kernel(back, basis, moment, update, moment_next, turned):
+def flip_kernel(source, out):
+    step = 256
+    for i in range(0, source.shape[0], step):
+        for j in range(0, source.shape[1], step):
+            out[j : j + step, i : i + step] = source[i : i + step, j : j + step].T
+
+
+def flip(basis):
+    return pl.pallas_call(
+        flip_kernel,
+        in_specs=[VMEM],
+        out_specs=VMEM,
+        out_shape=jax.ShapeDtypeStruct(basis.shape, basis.dtype),
+        compiler_params=limit(8),
+        cost_estimate=pl.CostEstimate(flops=0, bytes_accessed=4 * basis.size, transcendentals=0),
+        name="flip",
+    )(basis)
+
+
+def update_kernel(back, basis, moment, update, moment_next, turned, fresh, leave):
     count, _, _, width = back.shape
     for i in range(count):
         at = slice(i * width, (i + 1) * width)
         turned[:, at] = back[i, 0]
         rotated = back[i, 1].astype(f32)
-        moment_next[:, at] = ema_decay * moment[:, at] + (1.0 - ema_decay) * rotated * rotated
+        fresh[i] = ema_decay * moment[:, at] + (1.0 - ema_decay) * rotated * rotated
+        pltpu.make_async_copy(fresh.at[i], moment_next.at[:, i, 0], leave.at[i]).start()
     step = 256
-    for i in range(0, basis.shape[0], step):
-        update[:, i : i + step] = lax.dot_general(
-            turned[...], basis[i : i + step], (((1,), (1,)), ((), ())), preferred_element_type=f32
+    for i in range(0, basis.shape[1], step):
+        update[:, i : i + step] = jnp.dot(
+            turned[...], basis[:, i : i + step], preferred_element_type=f32
         ).astype(bf16)
+    for i in range(count):
+        pltpu.make_async_copy(fresh.at[i], moment_next.at[:, i, 0], leave.at[i]).wait()
 
 
 def finish(back, basis, moments):
     rows, order = moments.shape
+    count = back.shape[0]
     return pl.pallas_call(
         update_kernel,
         in_specs=[VMEM] * 3,
-        out_specs=[VMEM] * 2,
+        out_specs=[VMEM, ANY],
         out_shape=[
             jax.ShapeDtypeStruct((rows, order), bf16),
-            jax.ShapeDtypeStruct((rows, order), f32),
-        ],
-        scratch_shapes=[pltpu.VMEM((rows, order), bf16)],
+            jax.ShapeDtypeStruct((rows, count, 1, order // count), f32),
+        ],
+        scratch_shapes=[
+            pltpu.VMEM((rows, order), bf16),
+            pltpu.VMEM((count, rows, order // count), f32),
+            pltpu.SemaphoreType.DMA((count,)),
+        ],
         compiler_params=limit(16),
         name="finish",
     )(back, basis, moments)
@@ -215,16 +242,17 @@
         near += [a, b]
     near.append(lax.ppermute(a, "row", up))
     half = half_rotate(parts, in_basis[0], flat, count)
-    half, near = lax.optimization_barrier((half, near))
+    first, near = lax.optimization_barrier((half, near))
     held = stack(near)
     quarters = [held]
     for pairs in (y_next, y_last, x_swap):
         quarters.append(lax.ppermute(held, "col", pairs))
     quarters += [lax.ppermute(x, "row", swap) for x in quarters]
     half = lax.all_to_all(half, "row", split_axis=0, concat_axis=0, tiled=True)
+    half, flipped = lax.optimization_barrier((half, flip(lax.optimization_barrier((in_basis[0], held))[0])))
     back = rotate(place, half, quarters)
     back = lax.all_to_all(back, "row", split_axis=0, concat_axis=0, tiled=True)
-    update, new_moments = finish(back, in_basis[0], flat)
+    update, new_moments = finish(back, flipped, flat)
     return new_moments.reshape(1, rows, 1, order), update.reshape(1, rows, 1, order)
 
 

time: 131 us -> 125 us (0.954)
  waiting for transfers between devices: 25.8 us -> 16.8 us
  Pallas kernels: 16.4 us -> 18.4 us
    all_to_all x1, waiting for transfers between devices: 11.6 us -> 2.49 us  [shards(): half = lax.all_to_all(half, 'row', split_axis=0, concat_axis=0, tiled=True)]
    pallas_call x1 -> x2, Pallas kernels: 3.91 us -> 5.45 us  [the longest x1 3.04 us: finish(): pl.pallas_call(update_kernel, in_specs=[VMEM] * 3, out_specs=[VMEM, ANY],...]
    unnamed x9 -> x12, local copies, waits for them, and re-layouts: 9.49 us -> 10.7 us
  transfers between devices with their start and end apart: 16 -> 16, of which waited for: 7 -> 7; matrix products, arithmetic and copies ran while one was open for 1% -> 1% of each run, Pallas kernels for 3% -> 5%
where the time goes in v3:
time: 125 us
  starting transfers between devices  46.2 us (37%)
  blocking collectives  31.9 us (26%)
  Pallas kernels  18.4 us (15%)
  waiting for transfers between devices  16.8 us (13%)
  local copies, waits for them, and re-layouts  10.7 us (9%)
    all_to_all x1, blocking collectives, shards(): back = lax.all_to_all(back, 'row', split_axis=0, concat_axis=0, tiled=True)  31.9 us
    ppermute x4, starting transfers between devices, shards(): quarters += [lax.ppermute(x, 'row', swap) for x in quarters]  11.8 us
    unnamed x12, local copies, waits for them, and re-layouts  10.7 us
    all_to_all x1, starting transfers between devices, shards(): half = lax.all_to_all(half, 'row', split_axis=0, concat_axis=0, tiled=True)  10.4 us
    pallas_call x1, Pallas kernels, rotate(): pl.pallas_call(rotate_kernel, in_specs=[SMEM, VMEM] + [ANY] * 8, out_spec...  7.72 us
    all_to_all x1, starting transfers between devices, shards(): lax.all_to_all(sent, ('dp', 'col'), split_axis=0, concat_axis=0, tiled=True)  7.58 us
    ppermute x2, starting transfers between devices, shards(): a, b = (lax.ppermute(own, 'row', up), lax.ppermute(own, 'row', down))  5.66 us
    ppermute x3, starting transfers between devices, shards(): quarters.append(lax.ppermute(held, 'col', pairs))  5.4 us
  transfers between devices with their start and end apart: 16, of which 7 were waited for; matrix products, arithmetic and copies ran while one was open for 1% of the time, Pallas kernels for 5%

profile of v3, /device:TPU:1, one launch (start us, length us, event | category | flops | bytes accessed | tf_op | source)
XLA Modules:
  0.0 125.0 jit_solution(346135320920247600)
XLA Ops:
  0.6 0.0 copy-start
  0.6 2.5 %copy.7 = bf16[1,2,128,8,256]{4,2,3,1,0:T(8,128)(2,1)} copy(bf16[1,2,128,8,256]{4,3,2,1,0:T(8,128)(2,1)} %param.4) | data formatting | bytes 2097152 | tf_op args[0]
  3.1 7.6 %all-to-all-start = ((bf16[16,128,256]{2,1,0:T(8,128)(2,1)}), bf16[16,128,256]{2,1,0:T(8,128)(2,1)S(1)}, u32[]{:S(2)}, u32[]{:S(2)}) async-start(bf16[16,128,256]{2,1,0:T(8,128)(2,1)} %bitcast.5), calls=%async_computation | async-start | bytes 2097152 | tf_op jit(solution)/shard_map/all_to_all | solution.py:234
  10.8 5.7 %collective-permute-start.1 = (bf16[2,2,128,128]{3,2,1,0:T(8,128)(2,1)S(1)}, bf16[2,2,128,128]{3,2,1,0:T(8,128)(2,1)S(1)}, u32[]{:S(2)}, u32[]{:S(2)}) collective-permute-start(bf16[2,2,128,128]{3,2,1,0:T(8,128)(2,1)S(1)} %bitcast.21), channel_id=1, source_target_pairs={{16,0},{24,8},{32,16},{40,24},{48,32},{56,40},{64,48},{72,56},{80,... | collective-permute-start | bytes 393224 | tf_op jit(solution)/shard_map/ppermute | solution.py:231
  16.4 1.6 %copy.11 = f32[1,128,1,2048]{3,1,2,0:T(8,128)S(1)} copy(f32[1,128,1,2048]{3,2,1,0:T(1,128)} %param.7) | data formatting | bytes 2097152
  18.0 0.4 collective-permute-done.1.refs_2_
  18.4 3.4 %collective-permute-done.refs_1_ = bf16[2,2,128,128]{3,2,1,0:T(8,128)(2,1)S(1)} collective-permute-done((bf16[2,2,128,128]{3,2,1,0:T(8,128)(2,1)S(1)}, bf16[2,2,128,128]{3,2,1,0:T(8,128)(2,1)S(1)}, u32[]{:S(2)}, u32[]{:S(2)}) %collective-permute-start) | collective-permute-done | bytes 131104 | tf_op jit(solution)/shard_map/ppermute | solution.py:231
  21.7 0.0 collective-permute-start.2
  21.7 2.7 %collective-permute-start.3 = (bf16[2,2,128,128]{3,2,1,0:T(8,128)(2,1)S(1)}, bf16[2,2,128,128]{3,2,1,0:T(8,128)(2,1)S(1)}, u32[]{:S(2)}, u32[]{:S(2)}) collective-permute-start(bf16[2,2,128,128]{3,2,1,0:T(8,128)(2,1)S(1)} %collective-permute-done.1.refs_2_), channel_id=1, source_target_pairs={{16,0},{24,8},{32,16},{40,24},{48,32},{56,40},{64,48},{72,56},{80,... | collective-permute-start | bytes 393224 | tf_op jit(solution)/shard_map/ppermute | solution.py:241
  24.4 2.6 %collective-permute-done.2.refs_3_ = bf16[2,2,128,128]{3,2,1,0:T(8,128)(2,1)S(1)} collective-permute-done((bf16[2,2,128,128]{3,2,1,0:T(8,128)(2,1)S(1)}, bf16[2,2,128,128]{3,2,1,0:T(8,128)(2,1)S(1)}, u32[]{:S(2)}, u32[]{:S(2)}) %collective-permute-start.2) | collective-permute-done | bytes 131104 | tf_op jit(solution)/shard_map/ppermute | solution.py:241
  27.1 2.7 %collective-permute-start.5 = (bf16[2,2,128,128]{3,2,1,0:T(8,128)(2,1)S(1)}, bf16[2,2,128,128]{3,2,1,0:T(8,128)(2,1)S(1)}, u32[]{:S(2)}, u32[]{:S(2)}) collective-permute-start(bf16[2,2,128,128]{3,2,1,0:T(8,128)(2,1)S(1)} %collective-permute-done.3.refs_4_), channel_id=1, source_target_pairs={{16,0},{24,8},{32,16},{40,24},{48,32},{56,40},{64,48},{72,56},{80,... | collective-permute-start | bytes 393224 | tf_op jit(solution)/shard_map/ppermute | solution.py:241
  29.7 2.3 %collective-permute-done.4.refs_5_ = bf16[2,2,128,128]{3,2,1,0:T(8,128)(2,1)S(1)} collective-permute-done((bf16[2,2,128,128]{3,2,1,0:T(8,128)(2,1)S(1)}, bf16[2,2,128,128]{3,2,1,0:T(8,128)(2,1)S(1)}, u32[]{:S(2)}, u32[]{:S(2)}) %collective-permute-start.4) | collective-permute-done | bytes 131104 | tf_op jit(solution)/shard_map/ppermute | solution.py:241
  32.1 4.2 %half_rotate.1 = bf16[16,2,128,128]{3,2,1,0:T(8,128)(2,1)S(1)} custom-call(bf16[2,8,128,256]{3,2,1,0:T(8,128)(2,1)S(1)} %bitcast.20, bf16[2048,2048]{1,0:T(8,128)(2,1)} %bitcast.16, f32[128,2048]{1,0:T(8,128)S(1)} %bitcast.18), custom_call_target="tpu_custom_call" | custom-call | flops 1073741824 | bytes 8388608 | tf_op jit(solution)/shard_map/half_rotate/pallas_call | solution.py:50
  36.4 0.0 copy-start.4
  36.4 0.9 collective-permute-done.6.refs_7_
  37.2 1.0 stack.17.refs_0_
  38.2 3.0 %collective-permute-start.9 = (bf16[8,2,2,128,128]{4,3,2,1,0:T(8,128)(2,1)S(1)}, bf16[8,2,2,128,128]{4,3,2,1,0:T(8,128)(2,1)}, u32[]{:S(2)}, u32[]{:S(2)}) collective-permute-start(bf16[8,2,2,128,128]{4,3,2,1,0:T(8,128)(2,1)S(1)} %stack.17.refs_0_), channel_id=1, source_target_pairs={{0,4},{1,5},{2,6},{3,7},{4,0},{5,1},{6,2},{7,3},{8,12},{9,13},{10,... | collective-permute-start | bytes 3145736 | tf_op jit(solution)/shard_map/ppermute | solution.py:249
  41.2 2.4 %collective-permute-start.8 = (bf16[8,2,2,128,128]{4,3,2,1,0:T(8,128)(2,1)S(1)}, bf16[8,2,2,128,128]{4,3,2,1,0:T(8,128)(2,1)}, u32[]{:S(2)}, u32[]{:S(2)}) collective-permute-start(bf16[8,2,2,128,128]{4,3,2,1,0:T(8,128)(2,1)S(1)} %stack.17.refs_0_), channel_id=1, source_target_pairs={{1,0},{2,1},{3,2},{0,3},{5,4},{6,5},{7,6},{4,7},{9,8},{10,9},{11,1... | collective-permute-start | bytes 3145736 | tf_op jit(solution)/shard_map/ppermute | solution.py:249
  43.6 10.4 %all-to-all-start.1 = ((bf16[16,2,128,128]{3,2,1,0:T(8,128)(2,1)}), bf16[16,2,128,128]{3,2,1,0:T(8,128)(2,1)}, u32[]{:S(2)}, u32[]{:S(2)}) async-start(bf16[16,2,128,128]{3,2,1,0:T(8,128)(2,1)} %copy-done.4), calls=%async_computation.1 | async-start | bytes 2097152 | tf_op jit(solution)/shard_map/all_to_all | solution.py:251
  54.0 0.4 collective-permute-start.10
  54.4 4.7 %collective-permute-done.9.refs_3_ = bf16[8,2,2,128,128]{4,3,2,1,0:T(8,128)(2,1)} collective-permute-done((bf16[8,2,2,128,128]{4,3,2,1,0:T(8,128)(2,1)S(1)}, bf16[8,2,2,128,128]{4,3,2,1,0:T(8,128)(2,1)}, u32[]{:S(2)}, u32[]{:S(2)}) %collective-permute-start.9) | collective-permute-done | bytes 1048608 | tf_op jit(solution)/shard_map/ppermute | solution.py:249
  59.1 6.4 %collective-permute-start.13 = (bf16[8,2,2,128,128]{4,3,2,1,0:T(8,128)(2,1)}, bf16[8,2,2,128,128]{4,3,2,1,0:T(8,128)(2,1)}, u32[]{:S(2)}, u32[]{:S(2)}) collective-permute-start(bf16[8,2,2,128,128]{4,3,2,1,0:T(8,128)(2,1)} %collective-permute-done.9.refs_3_), channel_id=1, source_target_pairs={{0,8},{8,0},{16,24},{24,16},{32,40},{40,32},{48,56},{56,48},{64,72... | collective-permute-start | bytes 3145736 | tf_op jit(solution)/shard_map/ppermute | solution.py:250
  65.5 1.5 %collective-permute-start.12 = (bf16[8,2,2,128,128]{4,3,2,1,0:T(8,128)(2,1)}, bf16[8,2,2,128,128]{4,3,2,1,0:T(8,128)(2,1)}, u32[]{:S(2)}, u32[]{:S(2)}) collective-permute-start(bf16[8,2,2,128,128]{4,3,2,1,0:T(8,128)(2,1)} %collective-permute-done.8.refs_2_), channel_id=1, source_target_pairs={{0,8},{8,0},{16,24},{24,16},{32,40},{40,32},{48,56},{56,48},{64,72... | collective-permute-start | bytes 3145736 | tf_op jit(solution)/shard_map/ppermute | solution.py:250
  67.0 3.5 %collective-permute-start.11 = (bf16[8,2,2,128,128]{4,3,2,1,0:T(8,128)(2,1)}, bf16[8,2,2,128,128]{4,3,2,1,0:T(8,128)(2,1)}, u32[]{:S(2)}, u32[]{:S(2)}) collective-permute-start(bf16[8,2,2,128,128]{4,3,2,1,0:T(8,128)(2,1)} %collective-permute-done.7.refs_1_), channel_id=1, source_target_pairs={{0,8},{8,0},{16,24},{24,16},{32,40},{40,32},{48,56},{56,48},{64,72... | collective-permute-start | bytes 3145736 | tf_op jit(solution)/shard_map/ppermute | solution.py:250
  70.5 0.1 pad_add_fusion.place
  70.6 3.4 %copy-done.3 = bf16[1,2048,2048]{2,1,0:T(8,128)(2,1)S(1)} copy-done((bf16[1,2048,2048]{2,1,0:T(8,128)(2,1)S(1)}, bf16[1,2048,2048]{2,1,0:T(8,128)(2,1)}, u32[]{:S(2)}) %copy-start.3) | copy-done | bytes 8388632
  74.0 2.4 %flip.1.basis = bf16[2048,2048]{1,0:T(8,128)(2,1)S(1)} custom-call(bf16[2048,2048]{1,0:T(8,128)(2,1)S(1)} %bitcast.17), custom_call_target="tpu_custom_call" | custom-call | bytes 16777216 | tf_op jit(solution)/shard_map/flip/pallas_call | solution.py:165
  76.4 3.2 %copy-done.1 = bf16[2048,2048]{1,0:T(8,128)(2,1)} copy-done((bf16[2048,2048]{1,0:T(8,128)(2,1)}, bf16[2048,2048]{1,0:T(8,128)(2,1)S(1)}, u32[]{:S(2)}) %copy-start.1) | copy-done | bytes 8388632
  79.6 2.5 %all-to-all-done.1.mine = bf16[16,2,128,128]{3,2,1,0:T(8,128)(2,1)} async-done(((bf16[16,2,128,128]{3,2,1,0:T(8,128)(2,1)}), bf16[16,2,128,128]{3,2,1,0:T(8,128)(2,1)}, u32[]{:S(2)}, u32[]{:S(2)}) %all-to-all-start.1) | async-done | bytes 1048608 | tf_op jit(solution)/shard_map/all_to_all | solution.py:251
  82.2 7.7 %rotate.1 = bf16[16,2,128,128]{3,2,1,0:T(8,128)(2,1)S(1)} custom-call(s32[3]{0:T(128)S(1)} %pad_add_fusion.place, bf16[16,2,128,128]{3,2,1,0:T(8,128)(2,1)} %all-to-all-done.1.mine, bf16[8,2,2,128,128]{4,3,2,1,0:T(8,128)(2,1)S(1)} %stack.17.refs_0_, bf16[8,2,2,128,128]{4,3,2,1,0:T(8,128)(2,1)} %collective-permute-done.7.refs_1_, ...), custom_call_target="tpu_custom_call" | custom-call | flops 4294967296 | bytes 33554432 | tf_op jit(solution)/shard_map/rotate/pallas_call | solution.py:140
  89.9 31.9 %all_to_all.15.back = bf16[16,2,128,128]{3,2,1,0:T(8,128)(2,1)S(1)} all-to-all(bf16[16,2,128,128]{3,2,1,0:T(8,128)(2,1)S(1)} %rotate.1), channel_id=1, replica_groups=mesh['dp'=2,'row'=16,'col'=8] {'row'}, dimensions={0} | all-to-all | bytes 2097152 | tf_op jit(solution)/shard_map/all_to_all | solution.py:254
  121.8 3.0 %finish.1 = (bf16[128,2048]{1,0:T(8,128)(2,1)}, f32[128,16,1,128]{3,2,1,0:T(1,128)}) custom-call(bf16[16,2,128,128]{3,2,1,0:T(8,128)(2,1)S(1)} %all_to_all.15.back, bf16[2048,2048]{1,0:T(8,128)(2,1)S(1)} %copy-done.2, f32[128,2048]{1,0:T(8,128)S(1)} %bitcast.19), custom_call_target="tpu_custom_call" | custom-call | tf_op jit(solution)/shard_map/finish/pallas_call | solution.py:196
  (20 shorter events, 0.1 us)
Async XLA Ops:
  0.6 10.1 %copy-start = (bf16[1,2048,128]{2,1,0:T(8,128)(2,1)S(1)}, bf16[1,2048,128]{2,1,0:T(8,128)(2,1)}, u32[]{:S(2)}) copy-start(bf16[1,2048,128]{2,1,0:T(8,128)(2,1)} %param.5) | copy-start | bytes 1572868
  3.1 29.0 %all-to-all-start = ((bf16[16,128,256]{2,1,0:T(8,128)(2,1)}), bf16[16,128,256]{2,1,0:T(8,128)(2,1)S(1)}, u32[]{:S(2)}, u32[]{:S(2)}) async-start(bf16[16,128,256]{2,1,0:T(8,128)(2,1)} %bitcast.5), calls=%async_computation | async-start | bytes 2097152 | tf_op jit(solution)/shard_map/all_to_all | solution.py:234
  10.8 7.6 %collective-permute-start.1 = (bf16[2,2,128,128]{3,2,1,0:T(8,128)(2,1)S(1)}, bf16[2,2,128,128]{3,2,1,0:T(8,128)(2,1)S(1)}, u32[]{:S(2)}, u32[]{:S(2)}) collective-permute-start(bf16[2,2,128,128]{3,2,1,0:T(8,128)(2,1)S(1)} %bitcast.21), channel_id=1, source_target_pairs={{16,0},{24,8},{32,16},{40,24},{48,32},{56,40},{64,48},{72,56},{80,... | collective-permute-start | bytes 393224 | tf_op jit(solution)/shard_map/ppermute | solution.py:231
  16.4 5.3 %collective-permute-start = (bf16[2,2,128,128]{3,2,1,0:T(8,128)(2,1)S(1)}, bf16[2,2,128,128]{3,2,1,0:T(8,128)(2,1)S(1)}, u32[]{:S(2)}, u32[]{:S(2)}) collective-permute-start(bf16[2,2,128,128]{3,2,1,0:T(8,128)(2,1)S(1)} %bitcast.22), channel_id=1, source_target_pairs={{0,16},{8,24},{16,32},{24,40},{32,48},{40,56},{48,64},{56,72},{64,... | collective-permute-start | bytes 393224 | tf_op jit(solution)/shard_map/ppermute | solution.py:231
  21.7 5.3 %collective-permute-start.2 = (bf16[2,2,128,128]{3,2,1,0:T(8,128)(2,1)S(1)}, bf16[2,2,128,128]{3,2,1,0:T(8,128)(2,1)S(1)}, u32[]{:S(2)}, u32[]{:S(2)}) collective-permute-start(bf16[2,2,128,128]{3,2,1,0:T(8,128)(2,1)S(1)} %collective-permute-done.refs_1_), channel_id=1, source_target_pairs={{0,16},{8,24},{16,32},{24,40},{32,48},{40,56},{48,64},{56,72},{64,... | collective-permute-start | bytes 393224 | tf_op jit(solution)/shard_map/ppermute | solution.py:241
  21.7 5.3 %collective-permute-start.3 = (bf16[2,2,128,128]{3,2,1,0:T(8,128)(2,1)S(1)}, bf16[2,2,128,128]{3,2,1,0:T(8,128)(2,1)S(1)}, u32[]{:S(2)}, u32[]{:S(2)}) collective-permute-start(bf16[2,2,128,128]{3,2,1,0:T(8,128)(2,1)S(1)} %collective-permute-done.1.refs_2_), channel_id=1, source_target_pairs={{16,0},{24,8},{32,16},{40,24},{48,32},{56,40},{64,48},{72,56},{80,... | collective-permute-start | bytes 393224 | tf_op jit(solution)/shard_map/ppermute | solution.py:241
  27.1 5.0 %collective-permute-start.4 = (bf16[2,2,128,128]{3,2,1,0:T(8,128)(2,1)S(1)}, bf16[2,2,128,128]{3,2,1,0:T(8,128)(2,1)S(1)}, u32[]{:S(2)}, u32[]{:S(2)}) collective-permute-start(bf16[2,2,128,128]{3,2,1,0:T(8,128)(2,1)S(1)} %collective-permute-done.2.refs_3_), channel_id=1, source_target_pairs={{0,16},{8,24},{16,32},{24,40},{32,48},{40,56},{48,64},{56,72},{64,... | collective-permute-start | bytes 393224 | tf_op jit(solution)/shard_map/ppermute | solution.py:241
  27.1 9.3 %collective-permute-start.5 = (bf16[2,2,128,128]{3,2,1,0:T(8,128)(2,1)S(1)}, bf16[2,2,128,128]{3,2,1,0:T(8,128)(2,1)S(1)}, u32[]{:S(2)}, u32[]{:S(2)}) collective-permute-start(bf16[2,2,128,128]{3,2,1,0:T(8,128)(2,1)S(1)} %collective-permute-done.3.refs_4_), channel_id=1, source_target_pairs={{16,0},{24,8},{32,16},{40,24},{48,32},{56,40},{64,48},{72,56},{80,... | collective-permute-start | bytes 393224 | tf_op jit(solution)/shard_map/ppermute | solution.py:241
  32.1 5.1 %collective-permute-start.6 = (bf16[2,2,128,128]{3,2,1,0:T(8,128)(2,1)S(1)}, bf16[2,2,128,128]{3,2,1,0:T(8,128)(2,1)}, u32[]{:S(2)}, u32[]{:S(2)}) collective-permute-start(bf16[2,2,128,128]{3,2,1,0:T(8,128)(2,1)S(1)} %collective-permute-done.4.refs_5_), channel_id=1, source_target_pairs={{0,16},{8,24},{16,32},{24,40},{32,48},{40,56},{48,64},{56,72},{64,... | collective-permute-start | bytes 393224 | tf_op jit(solution)/shard_map/ppermute | solution.py:243
  36.4 7.3 %copy-start.4 = (bf16[16,2,128,128]{3,2,1,0:T(8,128)(2,1)}, bf16[16,2,128,128]{3,2,1,0:T(8,128)(2,1)S(1)}, u32[]{:S(2)}) copy-start(bf16[16,2,128,128]{3,2,1,0:T(8,128)(2,1)S(1)} %half_rotate.1) | copy-start | bytes 3145732
  38.2 20.9 %collective-permute-start.9 = (bf16[8,2,2,128,128]{4,3,2,1,0:T(8,128)(2,1)S(1)}, bf16[8,2,2,128,128]{4,3,2,1,0:T(8,128)(2,1)}, u32[]{:S(2)}, u32[]{:S(2)}) collective-permute-start(bf16[8,2,2,128,128]{4,3,2,1,0:T(8,128)(2,1)S(1)} %stack.17.refs_0_), channel_id=1, source_target_pairs={{0,4},{1,5},{2,6},{3,7},{4,0},{5,1},{6,2},{7,3},{8,12},{9,13},{10,... | collective-permute-start | bytes 3145736 | tf_op jit(solution)/shard_map/ppermute | solution.py:249
  41.2 24.3 %collective-permute-start.8 = (bf16[8,2,2,128,128]{4,3,2,1,0:T(8,128)(2,1)S(1)}, bf16[8,2,2,128,128]{4,3,2,1,0:T(8,128)(2,1)}, u32[]{:S(2)}, u32[]{:S(2)}) collective-permute-start(bf16[8,2,2,128,128]{4,3,2,1,0:T(8,128)(2,1)S(1)} %stack.17.refs_0_), channel_id=1, source_target_pairs={{1,0},{2,1},{3,2},{0,3},{5,4},{6,5},{7,6},{4,7},{9,8},{10,9},{11,1... | collective-permute-start | bytes 3145736 | tf_op jit(solution)/shard_map/ppermute | solution.py:249
  43.6 23.4 %collective-permute-start.7 = (bf16[8,2,2,128,128]{4,3,2,1,0:T(8,128)(2,1)S(1)}, bf16[8,2,2,128,128]{4,3,2,1,0:T(8,128)(2,1)}, u32[]{:S(2)}, u32[]{:S(2)}) collective-permute-start(bf16[8,2,2,128,128]{4,3,2,1,0:T(8,128)(2,1)S(1)} %stack.17.refs_0_), channel_id=1, source_target_pairs={{0,1},{1,2},{2,3},{3,0},{4,5},{5,6},{6,7},{7,4},{8,9},{9,10},{10,1... | collective-permute-start | bytes 3145736 | tf_op jit(solution)/shard_map/ppermute | solution.py:249
  43.6 38.5 %all-to-all-start.1 = ((bf16[16,2,128,128]{3,2,1,0:T(8,128)(2,1)}), bf16[16,2,128,128]{3,2,1,0:T(8,128)(2,1)}, u32[]{:S(2)}, u32[]{:S(2)}) async-start(bf16[16,2,128,128]{3,2,1,0:T(8,128)(2,1)} %copy-done.4), calls=%async_computation.1 | async-start | bytes 2097152 | tf_op jit(solution)/shard_map/all_to_all | solution.py:251
  54.0 28.1 %collective-permute-start.10 = (bf16[8,2,2,128,128]{4,3,2,1,0:T(8,128)(2,1)S(1)}, bf16[8,2,2,128,128]{4,3,2,1,0:T(8,128)(2,1)}, u32[]{:S(2)}, u32[]{:S(2)}) collective-permute-start(bf16[8,2,2,128,128]{4,3,2,1,0:T(8,128)(2,1)S(1)} %stack.17.refs_0_), channel_id=1, source_target_pairs={{0,8},{8,0},{16,24},{24,16},{32,40},{40,32},{48,56},{56,48},{64,72... | collective-permute-start | bytes 3145736 | tf_op jit(solution)/shard_map/ppermute | solution.py:250
  59.1 23.1 %collective-permute-start.13 = (bf16[8,2,2,128,128]{4,3,2,1,0:T(8,128)(2,1)}, bf16[8,2,2,128,128]{4,3,2,1,0:T(8,128)(2,1)}, u32[]{:S(2)}, u32[]{:S(2)}) collective-permute-start(bf16[8,2,2,128,128]{4,3,2,1,0:T(8,128)(2,1)} %collective-permute-done.9.refs_3_), channel_id=1, source_target_pairs={{0,8},{8,0},{16,24},{24,16},{32,40},{40,32},{48,56},{56,48},{64,72... | collective-permute-start | bytes 3145736 | tf_op jit(solution)/shard_map/ppermute | solution.py:250
  65.5 16.7 %collective-permute-start.12 = (bf16[8,2,2,128,128]{4,3,2,1,0:T(8,128)(2,1)}, bf16[8,2,2,128,128]{4,3,2,1,0:T(8,128)(2,1)}, u32[]{:S(2)}, u32[]{:S(2)}) collective-permute-start(bf16[8,2,2,128,128]{4,3,2,1,0:T(8,128)(2,1)} %collective-permute-done.8.refs_2_), channel_id=1, source_target_pairs={{0,8},{8,0},{16,24},{24,16},{32,40},{40,32},{48,56},{56,48},{64,72... | collective-permute-start | bytes 3145736 | tf_op jit(solution)/shard_map/ppermute | solution.py:250
  67.0 15.2 %collective-permute-start.11 = (bf16[8,2,2,128,128]{4,3,2,1,0:T(8,128)(2,1)}, bf16[8,2,2,128,128]{4,3,2,1,0:T(8,128)(2,1)}, u32[]{:S(2)}, u32[]{:S(2)}) collective-permute-start(bf16[8,2,2,128,128]{4,3,2,1,0:T(8,128)(2,1)} %collective-permute-done.7.refs_1_), channel_id=1, source_target_pairs={{0,8},{8,0},{16,24},{24,16},{32,40},{40,32},{48,56},{56,48},{64,72... | collective-permute-start | bytes 3145736 | tf_op jit(solution)/shard_map/ppermute | solution.py:250
  70.6 3.4 %copy-start.3 = (bf16[1,2048,2048]{2,1,0:T(8,128)(2,1)S(1)}, bf16[1,2048,2048]{2,1,0:T(8,128)(2,1)}, u32[]{:S(2)}) copy-start(bf16[1,2048,2048]{2,1,0:T(8,128)(2,1)} %param.6) | copy-start | bytes 25165828
  76.4 3.3 %copy-start.1 = (bf16[2048,2048]{1,0:T(8,128)(2,1)}, bf16[2048,2048]{1,0:T(8,128)(2,1)S(1)}, u32[]{:S(2)}) copy-start(bf16[2048,2048]{1,0:T(8,128)(2,1)S(1)} %flip.1.basis) | copy-start | bytes 25165828
  82.1 39.6 %copy-start.2 = (bf16[2048,2048]{1,0:T(8,128)(2,1)S(1)}, bf16[2048,2048]{1,0:T(8,128)(2,1)}, u32[]{:S(2)}) copy-start(bf16[2048,2048]{1,0:T(8,128)(2,1)} %copy-done.1) | copy-start | bytes 25165828

commit v4 on v3

--- a/solution.py
+++ b/solution.py
@@ -240,7 +240,7 @@
     for _ in range(2):
         a, b = lax.ppermute(a, "row", up), lax.ppermute(b, "row", down)
         near += [a, b]
-    near.append(lax.ppermute(a, "row", up))
+    near.append(lax.ppermute(near[3], "row", [(i, (i + 4) % count) for i in range(count)]))
     half = half_rotate(parts, in_basis[0], flat, count)
     first, near = lax.optimization_barrier((half, near))
     held = stack(near)

time: 125 us -> 121 us (0.968)
  starting transfers between devices: 46.2 us -> 43.6 us
  waiting for transfers between devices: 16.8 us -> 14.8 us
    ppermute x3, waiting for transfers between devices: 4.66 us -> 7.28 us  [shards(): quarters.append(lax.ppermute(held, 'col', pairs))]
    ppermute x4, waiting for transfers between devices: 5 us -> 2.65 us  [shards(): a, b = (lax.ppermute(a, 'row', up), lax.ppermute(b, 'row', down))]
    all_to_all x1, starting transfers between devices: 10.4 us -> 9.03 us  [shards(): half = lax.all_to_all(half, 'row', split_axis=0, concat_axis=0, tiled=True)]
    all_to_all x1, waiting for transfers between devices: 2.49 us -> 1.09 us  [shards(): half = lax.all_to_all(half, 'row', split_axis=0, concat_axis=0, tiled=True)]
  transfers between devices with their start and end apart: 16 -> 16, of which waited for: 7 -> 5; matrix products, arithmetic and copies ran while one was open for 1% -> 1% of each run, Pallas kernels for 5% -> 6%
where the time goes in v4:
time: 121 us
  starting transfers between devices  43.6 us (36%)
  blocking collectives  31.9 us (26%)
  Pallas kernels  18.5 us (15%)
  waiting for transfers between devices  14.8 us (12%)
  local copies, waits for them, and re-layouts  10.7 us (9%)
    all_to_all x1, blocking collectives, shards(): back = lax.all_to_all(back, 'row', split_axis=0, concat_axis=0, tiled=True)  31.9 us
    unnamed x12, local copies, waits for them, and re-layouts  10.7 us
    ppermute x4, starting transfers between devices, shards(): quarters += [lax.ppermute(x, 'row', swap) for x in quarters]  10.6 us
    all_to_all x1, starting transfers between devices, shards(): half = lax.all_to_all(half, 'row', split_axis=0, concat_axis=0, tiled=True)  9.03 us
    pallas_call x1, Pallas kernels, rotate(): pl.pallas_call(rotate_kernel, in_specs=[SMEM, VMEM] + [ANY] * 8, out_spec...  7.72 us
    all_to_all x1, starting transfers between devices, shards(): lax.all_to_all(sent, ('dp', 'col'), split_axis=0, concat_axis=0, tiled=True)  7.58 us
    ppermute x3, waiting for transfers between devices, shards(): quarters.append(lax.ppermute(held, 'col', pairs))  7.28 us
    ppermute x2, starting transfers between devices, shards(): a, b = (lax.ppermute(own, 'row', up), lax.ppermute(own, 'row', down))  5.66 us
  transfers between devices with their start and end apart: 16, of which 5 were waited for; matrix products, arithmetic and copies ran while one was open for 1% of the time, Pallas kernels for 6%

profile of v4, /device:TPU:1, one launch (start us, length us, event | category | flops | bytes accessed | tf_op | source)
XLA Modules:
  0.0 120.6 jit_solution(13586720518194125605)
XLA Ops:
  0.6 0.0 copy-start
  0.6 2.5 %copy.7 = bf16[1,2,128,8,256]{4,2,3,1,0:T(8,128)(2,1)} copy(bf16[1,2,128,8,256]{4,3,2,1,0:T(8,128)(2,1)} %param.4) | data formatting | bytes 2097152 | tf_op args[0]
  3.1 7.6 %all-to-all-start = ((bf16[16,128,256]{2,1,0:T(8,128)(2,1)}), bf16[16,128,256]{2,1,0:T(8,128)(2,1)S(1)}, u32[]{:S(2)}, u32[]{:S(2)}) async-start(bf16[16,128,256]{2,1,0:T(8,128)(2,1)} %bitcast.5), calls=%async_computation | async-start | bytes 2097152 | tf_op jit(solution)/shard_map/all_to_all | solution.py:234
  10.8 5.7 %collective-permute-start.1 = (bf16[2,2,128,128]{3,2,1,0:T(8,128)(2,1)S(1)}, bf16[2,2,128,128]{3,2,1,0:T(8,128)(2,1)S(1)}, u32[]{:S(2)}, u32[]{:S(2)}) collective-permute-start(bf16[2,2,128,128]{3,2,1,0:T(8,128)(2,1)S(1)} %bitcast.21), channel_id=1, source_target_pairs={{16,0},{24,8},{32,16},{40,24},{48,32},{56,40},{64,48},{72,56},{80,... | collective-permute-start | bytes 393224 | tf_op jit(solution)/shard_map/ppermute | solution.py:231
  16.4 1.6 %copy.11 = f32[1,128,1,2048]{3,1,2,0:T(8,128)S(1)} copy(f32[1,128,1,2048]{3,2,1,0:T(1,128)} %param.7) | data formatting | bytes 2097152
  18.0 0.4 collective-permute-done.1.refs_2_
  18.4 3.4 %collective-permute-done.refs_1_ = bf16[2,2,128,128]{3,2,1,0:T(8,128)(2,1)S(1)} collective-permute-done((bf16[2,2,128,128]{3,2,1,0:T(8,128)(2,1)S(1)}, bf16[2,2,128,128]{3,2,1,0:T(8,128)(2,1)S(1)}, u32[]{:S(2)}, u32[]{:S(2)}) %collective-permute-start) | collective-permute-done | bytes 131104 | tf_op jit(solution)/shard_map/ppermute | solution.py:231
  21.7 0.0 collective-permute-start.2
  21.7 2.7 %collective-permute-start.3 = (bf16[2,2,128,128]{3,2,1,0:T(8,128)(2,1)S(1)}, bf16[2,2,128,128]{3,2,1,0:T(8,128)(2,1)S(1)}, u32[]{:S(2)}, u32[]{:S(2)}) collective-permute-start(bf16[2,2,128,128]{3,2,1,0:T(8,128)(2,1)S(1)} %collective-permute-done.1.refs_2_), channel_id=1, source_target_pairs={{16,0},{24,8},{32,16},{40,24},{48,32},{56,40},{64,48},{72,56},{80,... | collective-permute-start | bytes 393224 | tf_op jit(solution)/shard_map/ppermute | solution.py:241
  24.4 2.6 %collective-permute-done.2.refs_3_ = bf16[2,2,128,128]{3,2,1,0:T(8,128)(2,1)S(1)} collective-permute-done((bf16[2,2,128,128]{3,2,1,0:T(8,128)(2,1)S(1)}, bf16[2,2,128,128]{3,2,1,0:T(8,128)(2,1)S(1)}, u32[]{:S(2)}, u32[]{:S(2)}) %collective-permute-start.2) | collective-permute-done | bytes 131104 | tf_op jit(solution)/shard_map/ppermute | solution.py:241
  27.1 0.0 collective-permute-start.4
  27.1 0.0 collective-permute-done.3.refs_4_
  27.1 2.7 %collective-permute-start.5 = (bf16[2,2,128,128]{3,2,1,0:T(8,128)(2,1)S(1)}, bf16[2,2,128,128]{3,2,1,0:T(8,128)(2,1)}, u32[]{:S(2)}, u32[]{:S(2)}) collective-permute-start(bf16[2,2,128,128]{3,2,1,0:T(8,128)(2,1)S(1)} %collective-permute-done.3.refs_4_), channel_id=1, source_target_pairs={{16,0},{24,8},{32,16},{40,24},{48,32},{56,40},{64,48},{72,56},{80,... | collective-permute-start | bytes 393224 | tf_op jit(solution)/shard_map/ppermute | solution.py:241
  29.8 4.2 %half_rotate.1 = bf16[16,2,128,128]{3,2,1,0:T(8,128)(2,1)S(1)} custom-call(bf16[2,8,128,256]{3,2,1,0:T(8,128)(2,1)S(1)} %bitcast.20, bf16[2048,2048]{1,0:T(8,128)(2,1)} %bitcast.16, f32[128,2048]{1,0:T(8,128)S(1)} %bitcast.18), custom_call_target="tpu_custom_call" | custom-call | flops 1073741824 | bytes 8388608 | tf_op jit(solution)/shard_map/half_rotate/pallas_call | solution.py:50
  34.0 0.0 copy-start.4
  34.0 1.1 stack.17.refs_0_
  35.2 3.0 %collective-permute-start.9 = (bf16[8,2,2,128,128]{4,3,2,1,0:T(8,128)(2,1)S(1)}, bf16[8,2,2,128,128]{4,3,2,1,0:T(8,128)(2,1)}, u32[]{:S(2)}, u32[]{:S(2)}) collective-permute-start(bf16[8,2,2,128,128]{4,3,2,1,0:T(8,128)(2,1)S(1)} %stack.17.refs_0_), channel_id=1, source_target_pairs={{0,4},{1,5},{2,6},{3,7},{4,0},{5,1},{6,2},{7,3},{8,12},{9,13},{10,... | collective-permute-start | bytes 3145736 | tf_op jit(solution)/shard_map/ppermute | solution.py:249
  38.2 2.5 %collective-permute-start.8 = (bf16[8,2,2,128,128]{4,3,2,1,0:T(8,128)(2,1)S(1)}, bf16[8,2,2,128,128]{4,3,2,1,0:T(8,128)(2,1)}, u32[]{:S(2)}, u32[]{:S(2)}) collective-permute-start(bf16[8,2,2,128,128]{4,3,2,1,0:T(8,128)(2,1)S(1)} %stack.17.refs_0_), channel_id=1, source_target_pairs={{1,0},{2,1},{3,2},{0,3},{5,4},{6,5},{7,6},{4,7},{9,8},{10,9},{11,1... | collective-permute-start | bytes 3145736 | tf_op jit(solution)/shard_map/ppermute | solution.py:249
  40.6 9.0 %all-to-all-start.1 = ((bf16[16,2,128,128]{3,2,1,0:T(8,128)(2,1)}), bf16[16,2,128,128]{3,2,1,0:T(8,128)(2,1)}, u32[]{:S(2)}, u32[]{:S(2)}) async-start(bf16[16,2,128,128]{3,2,1,0:T(8,128)(2,1)} %copy-done.4), calls=%async_computation.1 | async-start | bytes 2097152 | tf_op jit(solution)/shard_map/all_to_all | solution.py:251
  49.7 0.4 collective-permute-start.10
  50.0 7.3 %collective-permute-done.9.refs_3_ = bf16[8,2,2,128,128]{4,3,2,1,0:T(8,128)(2,1)} collective-permute-done((bf16[8,2,2,128,128]{4,3,2,1,0:T(8,128)(2,1)S(1)}, bf16[8,2,2,128,128]{4,3,2,1,0:T(8,128)(2,1)}, u32[]{:S(2)}, u32[]{:S(2)}) %collective-permute-start.9) | collective-permute-done | bytes 1048608 | tf_op jit(solution)/shard_map/ppermute | solution.py:249
  57.3 5.2 %collective-permute-start.13 = (bf16[8,2,2,128,128]{4,3,2,1,0:T(8,128)(2,1)}, bf16[8,2,2,128,128]{4,3,2,1,0:T(8,128)(2,1)}, u32[]{:S(2)}, u32[]{:S(2)}) collective-permute-start(bf16[8,2,2,128,128]{4,3,2,1,0:T(8,128)(2,1)} %collective-permute-done.9.refs_3_), channel_id=1, source_target_pairs={{0,8},{8,0},{16,24},{24,16},{32,40},{40,32},{48,56},{56,48},{64,72... | collective-permute-start | bytes 3145736 | tf_op jit(solution)/shard_map/ppermute | solution.py:250
  62.5 1.5 %collective-permute-start.12 = (bf16[8,2,2,128,128]{4,3,2,1,0:T(8,128)(2,1)}, bf16[8,2,2,128,128]{4,3,2,1,0:T(8,128)(2,1)}, u32[]{:S(2)}, u32[]{:S(2)}) collective-permute-start(bf16[8,2,2,128,128]{4,3,2,1,0:T(8,128)(2,1)} %collective-permute-done.8.refs_2_), channel_id=1, source_target_pairs={{0,8},{8,0},{16,24},{24,16},{32,40},{40,32},{48,56},{56,48},{64,72... | collective-permute-start | bytes 3145736 | tf_op jit(solution)/shard_map/ppermute | solution.py:250
  64.0 3.5 %collective-permute-start.11 = (bf16[8,2,2,128,128]{4,3,2,1,0:T(8,128)(2,1)}, bf16[8,2,2,128,128]{4,3,2,1,0:T(8,128)(2,1)}, u32[]{:S(2)}, u32[]{:S(2)}) collective-permute-start(bf16[8,2,2,128,128]{4,3,2,1,0:T(8,128)(2,1)} %collective-permute-done.7.refs_1_), channel_id=1, source_target_pairs={{0,8},{8,0},{16,24},{24,16},{32,40},{40,32},{48,56},{56,48},{64,72... | collective-permute-start | bytes 3145736 | tf_op jit(solution)/shard_map/ppermute | solution.py:250
  67.5 0.1 pad_add_fusion.place
  67.6 3.4 %copy-done.3 = bf16[1,2048,2048]{2,1,0:T(8,128)(2,1)S(1)} copy-done((bf16[1,2048,2048]{2,1,0:T(8,128)(2,1)S(1)}, bf16[1,2048,2048]{2,1,0:T(8,128)(2,1)}, u32[]{:S(2)}) %copy-start.3) | copy-done | bytes 8388632
  71.0 2.4 %flip.1.basis = bf16[2048,2048]{1,0:T(8,128)(2,1)S(1)} custom-call(bf16[2048,2048]{1,0:T(8,128)(2,1)S(1)} %bitcast.17), custom_call_target="tpu_custom_call" | custom-call | bytes 16777216 | tf_op jit(solution)/shard_map/flip/pallas_call | solution.py:165
  73.4 3.2 %copy-done.1 = bf16[2048,2048]{1,0:T(8,128)(2,1)} copy-done((bf16[2048,2048]{1,0:T(8,128)(2,1)}, bf16[2048,2048]{1,0:T(8,128)(2,1)S(1)}, u32[]{:S(2)}) %copy-start.1) | copy-done | bytes 8388632
  76.7 1.1 all-to-all-done.1.mine
  77.8 7.7 %rotate.1 = bf16[16,2,128,128]{3,2,1,0:T(8,128)(2,1)S(1)} custom-call(s32[3]{0:T(128)S(1)} %pad_add_fusion.place, bf16[16,2,128,128]{3,2,1,0:T(8,128)(2,1)} %all-to-all-done.1.mine, bf16[8,2,2,128,128]{4,3,2,1,0:T(8,128)(2,1)S(1)} %stack.17.refs_0_, bf16[8,2,2,128,128]{4,3,2,1,0:T(8,128)(2,1)} %collective-permute-done.7.refs_1_, ...), custom_call_target="tpu_custom_call" | custom-call | flops 4294967296 | bytes 33554432 | tf_op jit(solution)/shard_map/rotate/pallas_call | solution.py:140
  85.5 31.9 %all_to_all.15.back = bf16[16,2,128,128]{3,2,1,0:T(8,128)(2,1)S(1)} all-to-all(bf16[16,2,128,128]{3,2,1,0:T(8,128)(2,1)S(1)} %rotate.1), channel_id=1, replica_groups=mesh['dp'=2,'row'=16,'col'=8] {'row'}, dimensions={0} | all-to-all | bytes 2097152 | tf_op jit(solution)/shard_map/all_to_all | solution.py:254
  117.4 3.0 %finish.1 = (bf16[128,2048]{1,0:T(8,128)(2,1)}, f32[128,16,1,128]{3,2,1,0:T(1,128)}) custom-call(bf16[16,2,128,128]{3,2,1,0:T(8,128)(2,1)S(1)} %all_to_all.15.back, bf16[2048,2048]{1,0:T(8,128)(2,1)S(1)} %copy-done.2, f32[128,2048]{1,0:T(8,128)S(1)} %bitcast.19), custom_call_target="tpu_custom_call" | custom-call | tf_op jit(solution)/shard_map/finish/pallas_call | solution.py:196
  (20 shorter events, 0.1 us)
Async XLA Ops:
  0.6 10.1 %copy-start = (bf16[1,2048,128]{2,1,0:T(8,128)(2,1)S(1)}, bf16[1,2048,128]{2,1,0:T(8,128)(2,1)}, u32[]{:S(2)}) copy-start(bf16[1,2048,128]{2,1,0:T(8,128)(2,1)} %param.5) | copy-start | bytes 1572868
  3.1 26.6 %all-to-all-start = ((bf16[16,128,256]{2,1,0:T(8,128)(2,1)}), bf16[16,128,256]{2,1,0:T(8,128)(2,1)S(1)}, u32[]{:S(2)}, u32[]{:S(2)}) async-start(bf16[16,128,256]{2,1,0:T(8,128)(2,1)} %bitcast.5), calls=%async_computation | async-start | bytes 2097152 | tf_op jit(solution)/shard_map/all_to_all | solution.py:234
  10.8 7.6 %collective-permute-start.1 = (bf16[2,2,128,128]{3,2,1,0:T(8,128)(2,1)S(1)}, bf16[2,2,128,128]{3,2,1,0:T(8,128)(2,1)S(1)}, u32[]{:S(2)}, u32[]{:S(2)}) collective-permute-start(bf16[2,2,128,128]{3,2,1,0:T(8,128)(2,1)S(1)} %bitcast.21), channel_id=1, source_target_pairs={{16,0},{24,8},{32,16},{40,24},{48,32},{56,40},{64,48},{72,56},{80,... | collective-permute-start | bytes 393224 | tf_op jit(solution)/shard_map/ppermute | solution.py:231
  16.4 5.3 %collective-permute-start = (bf16[2,2,128,128]{3,2,1,0:T(8,128)(2,1)S(1)}, bf16[2,2,128,128]{3,2,1,0:T(8,128)(2,1)S(1)}, u32[]{:S(2)}, u32[]{:S(2)}) collective-permute-start(bf16[2,2,128,128]{3,2,1,0:T(8,128)(2,1)S(1)} %bitcast.22), channel_id=1, source_target_pairs={{0,16},{8,24},{16,32},{24,40},{32,48},{40,56},{48,64},{56,72},{64,... | collective-permute-start | bytes 393224 | tf_op jit(solution)/shard_map/ppermute | solution.py:231
  21.7 5.3 %collective-permute-start.2 = (bf16[2,2,128,128]{3,2,1,0:T(8,128)(2,1)S(1)}, bf16[2,2,128,128]{3,2,1,0:T(8,128)(2,1)S(1)}, u32[]{:S(2)}, u32[]{:S(2)}) collective-permute-start(bf16[2,2,128,128]{3,2,1,0:T(8,128)(2,1)S(1)} %collective-permute-done.refs_1_), channel_id=1, source_target_pairs={{0,16},{8,24},{16,32},{24,40},{32,48},{40,56},{48,64},{56,72},{64,... | collective-permute-start | bytes 393224 | tf_op jit(solution)/shard_map/ppermute | solution.py:241
  21.7 5.3 %collective-permute-start.3 = (bf16[2,2,128,128]{3,2,1,0:T(8,128)(2,1)S(1)}, bf16[2,2,128,128]{3,2,1,0:T(8,128)(2,1)S(1)}, u32[]{:S(2)}, u32[]{:S(2)}) collective-permute-start(bf16[2,2,128,128]{3,2,1,0:T(8,128)(2,1)S(1)} %collective-permute-done.1.refs_2_), channel_id=1, source_target_pairs={{16,0},{24,8},{32,16},{40,24},{48,32},{56,40},{64,48},{72,56},{80,... | collective-permute-start | bytes 393224 | tf_op jit(solution)/shard_map/ppermute | solution.py:241
  27.1 7.0 %collective-permute-start.6 = (bf16[2,2,128,128]{3,2,1,0:T(8,128)(2,1)S(1)}, bf16[2,2,128,128]{3,2,1,0:T(8,128)(2,1)S(1)}, u32[]{:S(2)}, u32[]{:S(2)}) collective-permute-start(bf16[2,2,128,128]{3,2,1,0:T(8,128)(2,1)S(1)} %collective-permute-done.2.refs_3_), channel_id=1, source_target_pairs={{0,32},{8,40},{16,48},{24,56},{32,64},{40,72},{48,80},{56,88},{64,... | collective-permute-start | bytes 393224 | tf_op jit(solution)/shard_map/ppermute | solution.py:243
  27.1 7.0 %collective-permute-start.4 = (bf16[2,2,128,128]{3,2,1,0:T(8,128)(2,1)S(1)}, bf16[2,2,128,128]{3,2,1,0:T(8,128)(2,1)S(1)}, u32[]{:S(2)}, u32[]{:S(2)}) collective-permute-start(bf16[2,2,128,128]{3,2,1,0:T(8,128)(2,1)S(1)} %collective-permute-done.2.refs_3_), channel_id=1, source_target_pairs={{0,16},{8,24},{16,32},{24,40},{32,48},{40,56},{48,64},{56,72},{64,... | collective-permute-start | bytes 393224 | tf_op jit(solution)/shard_map/ppermute | solution.py:241
  27.1 7.0 %collective-permute-start.5 = (bf16[2,2,128,128]{3,2,1,0:T(8,128)(2,1)S(1)}, bf16[2,2,128,128]{3,2,1,0:T(8,128)(2,1)}, u32[]{:S(2)}, u32[]{:S(2)}) collective-permute-start(bf16[2,2,128,128]{3,2,1,0:T(8,128)(2,1)S(1)} %collective-permute-done.3.refs_4_), channel_id=1, source_target_pairs={{16,0},{24,8},{32,16},{40,24},{48,32},{56,40},{64,48},{72,56},{80,... | collective-permute-start | bytes 393224 | tf_op jit(solution)/shard_map/ppermute | solution.py:241
  34.0 6.6 %copy-start.4 = (bf16[16,2,128,128]{3,2,1,0:T(8,128)(2,1)}, bf16[16,2,128,128]{3,2,1,0:T(8,128)(2,1)S(1)}, u32[]{:S(2)}) copy-start(bf16[16,2,128,128]{3,2,1,0:T(8,128)(2,1)S(1)} %half_rotate.1) | copy-start | bytes 3145732
  35.2 22.1 %collective-permute-start.9 = (bf16[8,2,2,128,128]{4,3,2,1,0:T(8,128)(2,1)S(1)}, bf16[8,2,2,128,128]{4,3,2,1,0:T(8,128)(2,1)}, u32[]{:S(2)}, u32[]{:S(2)}) collective-permute-start(bf16[8,2,2,128,128]{4,3,2,1,0:T(8,128)(2,1)S(1)} %stack.17.refs_0_), channel_id=1, source_target_pairs={{0,4},{1,5},{2,6},{3,7},{4,0},{5,1},{6,2},{7,3},{8,12},{9,13},{10,... | collective-permute-start | bytes 3145736 | tf_op jit(solution)/shard_map/ppermute | solution.py:249
  38.2 24.3 %collective-permute-start.8 = (bf16[8,2,2,128,128]{4,3,2,1,0:T(8,128)(2,1)S(1)}, bf16[8,2,2,128,128]{4,3,2,1,0:T(8,128)(2,1)}, u32[]{:S(2)}, u32[]{:S(2)}) collective-permute-start(bf16[8,2,2,128,128]{4,3,2,1,0:T(8,128)(2,1)S(1)} %stack.17.refs_0_), channel_id=1, source_target_pairs={{1,0},{2,1},{3,2},{0,3},{5,4},{6,5},{7,6},{4,7},{9,8},{10,9},{11,1... | collective-permute-start | bytes 3145736 | tf_op jit(solution)/shard_map/ppermute | solution.py:249
  40.6 23.4 %collective-permute-start.7 = (bf16[8,2,2,128,128]{4,3,2,1,0:T(8,128)(2,1)S(1)}, bf16[8,2,2,128,128]{4,3,2,1,0:T(8,128)(2,1)}, u32[]{:S(2)}, u32[]{:S(2)}) collective-permute-start(bf16[8,2,2,128,128]{4,3,2,1,0:T(8,128)(2,1)S(1)} %stack.17.refs_0_), channel_id=1, source_target_pairs={{0,1},{1,2},{2,3},{3,0},{4,5},{5,6},{6,7},{7,4},{8,9},{9,10},{10,1... | collective-permute-start | bytes 3145736 | tf_op jit(solution)/shard_map/ppermute | solution.py:249
  40.6 37.1 %all-to-all-start.1 = ((bf16[16,2,128,128]{3,2,1,0:T(8,128)(2,1)}), bf16[16,2,128,128]{3,2,1,0:T(8,128)(2,1)}, u32[]{:S(2)}, u32[]{:S(2)}) async-start(bf16[16,2,128,128]{3,2,1,0:T(8,128)(2,1)} %copy-done.4), calls=%async_computation.1 | async-start | bytes 2097152 | tf_op jit(solution)/shard_map/all_to_all | solution.py:251
  49.7 28.1 %collective-permute-start.10 = (bf16[8,2,2,128,128]{4,3,2,1,0:T(8,128)(2,1)S(1)}, bf16[8,2,2,128,128]{4,3,2,1,0:T(8,128)(2,1)}, u32[]{:S(2)}, u32[]{:S(2)}) collective-permute-start(bf16[8,2,2,128,128]{4,3,2,1,0:T(8,128)(2,1)S(1)} %stack.17.refs_0_), channel_id=1, source_target_pairs={{0,8},{8,0},{16,24},{24,16},{32,40},{40,32},{48,56},{56,48},{64,72... | collective-permute-start | bytes 3145736 | tf_op jit(solution)/shard_map/ppermute | solution.py:250
  57.3 20.5 %collective-permute-start.13 = (bf16[8,2,2,128,128]{4,3,2,1,0:T(8,128)(2,1)}, bf16[8,2,2,128,128]{4,3,2,1,0:T(8,128)(2,1)}, u32[]{:S(2)}, u32[]{:S(2)}) collective-permute-start(bf16[8,2,2,128,128]{4,3,2,1,0:T(8,128)(2,1)} %collective-permute-done.9.refs_3_), channel_id=1, source_target_pairs={{0,8},{8,0},{16,24},{24,16},{32,40},{40,32},{48,56},{56,48},{64,72... | collective-permute-start | bytes 3145736 | tf_op jit(solution)/shard_map/ppermute | solution.py:250
  62.5 15.3 %collective-permute-start.12 = (bf16[8,2,2,128,128]{4,3,2,1,0:T(8,128)(2,1)}, bf16[8,2,2,128,128]{4,3,2,1,0:T(8,128)(2,1)}, u32[]{:S(2)}, u32[]{:S(2)}) collective-permute-start(bf16[8,2,2,128,128]{4,3,2,1,0:T(8,128)(2,1)} %collective-permute-done.8.refs_2_), channel_id=1, source_target_pairs={{0,8},{8,0},{16,24},{24,16},{32,40},{40,32},{48,56},{56,48},{64,72... | collective-permute-start | bytes 3145736 | tf_op jit(solution)/shard_map/ppermute | solution.py:250
  64.0 13.8 %collective-permute-start.11 = (bf16[8,2,2,128,128]{4,3,2,1,0:T(8,128)(2,1)}, bf16[8,2,2,128,128]{4,3,2,1,0:T(8,128)(2,1)}, u32[]{:S(2)}, u32[]{:S(2)}) collective-permute-start(bf16[8,2,2,128,128]{4,3,2,1,0:T(8,128)(2,1)} %collective-permute-done.7.refs_1_), channel_id=1, source_target_pairs={{0,8},{8,0},{16,24},{24,16},{32,40},{40,32},{48,56},{56,48},{64,72... | collective-permute-start | bytes 3145736 | tf_op jit(solution)/shard_map/ppermute | solution.py:250
  67.6 3.4 %copy-start.3 = (bf16[1,2048,2048]{2,1,0:T(8,128)(2,1)S(1)}, bf16[1,2048,2048]{2,1,0:T(8,128)(2,1)}, u32[]{:S(2)}) copy-start(bf16[1,2048,2048]{2,1,0:T(8,128)(2,1)} %param.6) | copy-start | bytes 25165828
  73.4 3.3 %copy-start.1 = (bf16[2048,2048]{1,0:T(8,128)(2,1)}, bf16[2048,2048]{1,0:T(8,128)(2,1)S(1)}, u32[]{:S(2)}) copy-start(bf16[2048,2048]{1,0:T(8,128)(2,1)S(1)} %flip.1.basis) | copy-start | bytes 25165828
  77.8 39.6 %copy-start.2 = (bf16[2048,2048]{1,0:T(8,128)(2,1)S(1)}, bf16[2048,2048]{1,0:T(8,128)(2,1)}, u32[]{:S(2)}) copy-start(bf16[2048,2048]{1,0:T(8,128)(2,1)} %copy-done.1) | copy-start | bytes 25165828

commit v5 on v4

--- a/solution.py
+++ b/solution.py
@@ -154,20 +154,41 @@
     )(place, mine, *sources)
 
 
-def flip_kernel(source, out):
+def flip_kernel(source, out, held, turned, arrive, leave):
     step = 256
-    for i in range(0, source.shape[0], step):
+    spans = [pl.ds(i, step) for i in range(0, source.shape[0], step)]
+    ins = [
+        pltpu.make_async_copy(source.at[at], held.at[at], arrive.at[i]) for i, at in enumerate(spans)
+    ]
+    outs = [
+        pltpu.make_async_copy(turned.at[:, at], out.at[:, at], leave.at[i])
+        for i, at in enumerate(spans)
+    ]
+    for copy in ins:
+        copy.start()
+    for i in range(len(spans)):
+        ins[i].wait()
+        rows = slice(i * step, (i + 1) * step)
         for j in range(0, source.shape[1], step):
-            out[j : j + step, i : i + step] = source[i : i + step, j : j + step].T
+            turned[j : j + step, rows] = held[rows, j : j + step].T
+        outs[i].start()
+    for copy in outs:
+        copy.wait()
 
 
 def flip(basis):
     return pl.pallas_call(
         flip_kernel,
-        in_specs=[VMEM],
-        out_specs=VMEM,
+        in_specs=[ANY],
+        out_specs=ANY,
         out_shape=jax.ShapeDtypeStruct(basis.shape, basis.dtype),
-        compiler_params=limit(8),
+        scratch_shapes=[
+            pltpu.VMEM(basis.shape, basis.dtype),
+            pltpu.VMEM(basis.shape, basis.dtype),
+            pltpu.SemaphoreType.DMA((8,)),
+            pltpu.SemaphoreType.DMA((8,)),
+        ],
+        compiler_params=limit(50),
         cost_estimate=pl.CostEstimate(flops=0, bytes_accessed=4 * basis.size, transcendentals=0),
         name="flip",
     )(basis)

time: 121 us -> 121 us (level)
  local copies, waits for them, and re-layouts: 10.7 us -> 4.08 us
  Pallas kernels: 18.5 us -> 23.3 us
  waiting for transfers between devices: 14.8 us -> 16.7 us
    unnamed x12 -> x8, local copies, waits for them, and re-layouts: 10.7 us -> 4.07 us
    pallas_call x1, Pallas kernels: 2.41 us -> 7.11 us  [flip(): pl.pallas_call(flip_kernel, in_specs=[ANY], out_specs=ANY, out_shape=jax....]
    all_to_all x1, waiting for transfers between devices: 1.09 us -> 3.04 us  [shards(): half = lax.all_to_all(half, 'row', split_axis=0, concat_axis=0, tiled=True)]
  transfers between devices with their start and end apart: 16 -> 16, of which waited for: 5 -> 5; matrix products, arithmetic and copies ran while one was open for 1% -> 1% of each run, Pallas kernels for 6% -> 9%
where the time goes in v5:
time: 121 us
  starting transfers between devices  43.6 us (36%)
  blocking collectives  31.9 us (26%)
  Pallas kernels  23.3 us (19%)
  waiting for transfers between devices  16.7 us (14%)
  local copies, waits for them, and re-layouts  4.08 us (3%)
    all_to_all x1, blocking collectives, shards(): back = lax.all_to_all(back, 'row', split_axis=0, concat_axis=0, tiled=True)  31.9 us
    ppermute x4, starting transfers between devices, shards(): quarters += [lax.ppermute(x, 'row', swap) for x in quarters]  10.6 us
    all_to_all x1, starting transfers between devices, shards(): half = lax.all_to_all(half, 'row', split_axis=0, concat_axis=0, tiled=True)  9.04 us
    pallas_call x1, Pallas kernels, rotate(): pl.pallas_call(rotate_kernel, in_specs=[SMEM, VMEM] + [ANY] * 8, out_spec...  7.72 us
    all_to_all x1, starting transfers between devices, shards(): lax.all_to_all(sent, ('dp', 'col'), split_axis=0, concat_axis=0, tiled=True)  7.58 us
    ppermute x3, waiting for transfers between devices, shards(): quarters.append(lax.ppermute(held, 'col', pairs))  7.27 us
    pallas_call x1, Pallas kernels, flip(): pl.pallas_call(flip_kernel, in_specs=[ANY], out_specs=ANY, out_shape=jax....  7.11 us
    ppermute x2, starting transfers between devices, shards(): a, b = (lax.ppermute(own, 'row', up), lax.ppermute(own, 'row', down))  5.66 us
  transfers between devices with their start and end apart: 16, of which 5 were waited for; matrix products, arithmetic and copies ran while one was open for 1% of the time, Pallas kernels for 9%

profile of v5, /device:TPU:1, one launch (start us, length us, event | category | flops | bytes accessed | tf_op | source)
XLA Modules:
  0.0 120.6 jit_solution(6289310745568456790)
XLA Ops:
  0.6 0.0 copy-start
  0.6 2.5 %copy.7 = bf16[1,2,128,8,256]{4,2,3,1,0:T(8,128)(2,1)} copy(bf16[1,2,128,8,256]{4,3,2,1,0:T(8,128)(2,1)} %param.4) | data formatting | bytes 2097152 | tf_op args[0]
  3.1 7.6 %all-to-all-start = ((bf16[16,128,256]{2,1,0:T(8,128)(2,1)}), bf16[16,128,256]{2,1,0:T(8,128)(2,1)S(1)}, u32[]{:S(2)}, u32[]{:S(2)}) async-start(bf16[16,128,256]{2,1,0:T(8,128)(2,1)} %bitcast.5), calls=%async_computation | async-start | bytes 2097152 | tf_op jit(solution)/shard_map/all_to_all | solution.py:255
  10.8 5.7 %collective-permute-start.1 = (bf16[2,2,128,128]{3,2,1,0:T(8,128)(2,1)S(1)}, bf16[2,2,128,128]{3,2,1,0:T(8,128)(2,1)S(1)}, u32[]{:S(2)}, u32[]{:S(2)}) collective-permute-start(bf16[2,2,128,128]{3,2,1,0:T(8,128)(2,1)S(1)} %bitcast.19), channel_id=1, source_target_pairs={{16,0},{24,8},{32,16},{40,24},{48,32},{56,40},{64,48},{72,56},{80,... | collective-permute-start | bytes 393224 | tf_op jit(solution)/shard_map/ppermute | solution.py:252
  16.4 1.6 %copy.11 = f32[1,128,1,2048]{3,1,2,0:T(8,128)S(1)} copy(f32[1,128,1,2048]{3,2,1,0:T(1,128)} %param.7) | data formatting | bytes 2097152
  18.0 0.4 collective-permute-done.1.refs_2_
  18.4 3.4 %collective-permute-done.refs_1_ = bf16[2,2,128,128]{3,2,1,0:T(8,128)(2,1)S(1)} collective-permute-done((bf16[2,2,128,128]{3,2,1,0:T(8,128)(2,1)S(1)}, bf16[2,2,128,128]{3,2,1,0:T(8,128)(2,1)S(1)}, u32[]{:S(2)}, u32[]{:S(2)}) %collective-permute-start) | collective-permute-done | bytes 131104 | tf_op jit(solution)/shard_map/ppermute | solution.py:252
  21.7 0.0 collective-permute-start.2
  21.7 2.7 %collective-permute-start.3 = (bf16[2,2,128,128]{3,2,1,0:T(8,128)(2,1)S(1)}, bf16[2,2,128,128]{3,2,1,0:T(8,128)(2,1)S(1)}, u32[]{:S(2)}, u32[]{:S(2)}) collective-permute-start(bf16[2,2,128,128]{3,2,1,0:T(8,128)(2,1)S(1)} %collective-permute-done.1.refs_2_), channel_id=1, source_target_pairs={{16,0},{24,8},{32,16},{40,24},{48,32},{56,40},{64,48},{72,56},{80,... | collective-permute-start | bytes 393224 | tf_op jit(solution)/shard_map/ppermute | solution.py:262
  24.4 2.6 %collective-permute-done.2.refs_3_ = bf16[2,2,128,128]{3,2,1,0:T(8,128)(2,1)S(1)} collective-permute-done((bf16[2,2,128,128]{3,2,1,0:T(8,128)(2,1)S(1)}, bf16[2,2,128,128]{3,2,1,0:T(8,128)(2,1)S(1)}, u32[]{:S(2)}, u32[]{:S(2)}) %collective-permute-start.2) | collective-permute-done | bytes 131104 | tf_op jit(solution)/shard_map/ppermute | solution.py:262
  27.1 0.0 collective-permute-done.3.refs_4_
  27.1 2.7 %collective-permute-start.5 = (bf16[2,2,128,128]{3,2,1,0:T(8,128)(2,1)S(1)}, bf16[2,2,128,128]{3,2,1,0:T(8,128)(2,1)}, u32[]{:S(2)}, u32[]{:S(2)}) collective-permute-start(bf16[2,2,128,128]{3,2,1,0:T(8,128)(2,1)S(1)} %collective-permute-done.3.refs_4_), channel_id=1, source_target_pairs={{16,0},{24,8},{32,16},{40,24},{48,32},{56,40},{64,48},{72,56},{80,... | collective-permute-start | bytes 393224 | tf_op jit(solution)/shard_map/ppermute | solution.py:262
  29.7 0.0 all-to-all-done
  29.8 4.2 %half_rotate.1 = bf16[16,2,128,128]{3,2,1,0:T(8,128)(2,1)S(1)} custom-call(bf16[2,8,128,256]{3,2,1,0:T(8,128)(2,1)S(1)} %bitcast.18, bf16[2048,2048]{1,0:T(8,128)(2,1)} %bitcast.22, f32[128,2048]{1,0:T(8,128)S(1)} %bitcast.16), custom_call_target="tpu_custom_call" | custom-call | flops 1073741824 | bytes 8388608 | tf_op jit(solution)/shard_map/half_rotate/pallas_call | solution.py:50
  34.0 0.0 copy-start.2
  34.0 0.0 collective-permute-done.4.refs_5_
  34.0 0.0 collective-permute-done.5.refs_6_
  34.0 1.1 stack.17.refs_0_
  35.2 3.0 %collective-permute-start.9 = (bf16[8,2,2,128,128]{4,3,2,1,0:T(8,128)(2,1)S(1)}, bf16[8,2,2,128,128]{4,3,2,1,0:T(8,128)(2,1)}, u32[]{:S(2)}, u32[]{:S(2)}) collective-permute-start(bf16[8,2,2,128,128]{4,3,2,1,0:T(8,128)(2,1)S(1)} %stack.17.refs_0_), channel_id=1, source_target_pairs={{0,4},{1,5},{2,6},{3,7},{4,0},{5,1},{6,2},{7,3},{8,12},{9,13},{10,... | collective-permute-start | bytes 3145736 | tf_op jit(solution)/shard_map/ppermute | solution.py:270
  38.2 2.5 %collective-permute-start.8 = (bf16[8,2,2,128,128]{4,3,2,1,0:T(8,128)(2,1)S(1)}, bf16[8,2,2,128,128]{4,3,2,1,0:T(8,128)(2,1)}, u32[]{:S(2)}, u32[]{:S(2)}) collective-permute-start(bf16[8,2,2,128,128]{4,3,2,1,0:T(8,128)(2,1)S(1)} %stack.17.refs_0_), channel_id=1, source_target_pairs={{1,0},{2,1},{3,2},{0,3},{5,4},{6,5},{7,6},{4,7},{9,8},{10,9},{11,1... | collective-permute-start | bytes 3145736 | tf_op jit(solution)/shard_map/ppermute | solution.py:270
  40.6 9.0 %all-to-all-start.1 = ((bf16[16,2,128,128]{3,2,1,0:T(8,128)(2,1)}), bf16[16,2,128,128]{3,2,1,0:T(8,128)(2,1)}, u32[]{:S(2)}, u32[]{:S(2)}) async-start(bf16[16,2,128,128]{3,2,1,0:T(8,128)(2,1)} %copy-done.2), calls=%async_computation.1 | async-start | bytes 2097152 | tf_op jit(solution)/shard_map/all_to_all | solution.py:272
  49.7 0.4 collective-permute-start.10
  50.0 7.3 %collective-permute-done.9.refs_3_ = bf16[8,2,2,128,128]{4,3,2,1,0:T(8,128)(2,1)} collective-permute-done((bf16[8,2,2,128,128]{4,3,2,1,0:T(8,128)(2,1)S(1)}, bf16[8,2,2,128,128]{4,3,2,1,0:T(8,128)(2,1)}, u32[]{:S(2)}, u32[]{:S(2)}) %collective-permute-start.9) | collective-permute-done | bytes 1048608 | tf_op jit(solution)/shard_map/ppermute | solution.py:270
  57.3 5.2 %collective-permute-start.13 = (bf16[8,2,2,128,128]{4,3,2,1,0:T(8,128)(2,1)}, bf16[8,2,2,128,128]{4,3,2,1,0:T(8,128)(2,1)}, u32[]{:S(2)}, u32[]{:S(2)}) collective-permute-start(bf16[8,2,2,128,128]{4,3,2,1,0:T(8,128)(2,1)} %collective-permute-done.9.refs_3_), channel_id=1, source_target_pairs={{0,8},{8,0},{16,24},{24,16},{32,40},{40,32},{48,56},{56,48},{64,72... | collective-permute-start | bytes 3145736 | tf_op jit(solution)/shard_map/ppermute | solution.py:271
  62.5 1.5 %collective-permute-start.12 = (bf16[8,2,2,128,128]{4,3,2,1,0:T(8,128)(2,1)}, bf16[8,2,2,128,128]{4,3,2,1,0:T(8,128)(2,1)}, u32[]{:S(2)}, u32[]{:S(2)}) collective-permute-start(bf16[8,2,2,128,128]{4,3,2,1,0:T(8,128)(2,1)} %collective-permute-done.8.refs_2_), channel_id=1, source_target_pairs={{0,8},{8,0},{16,24},{24,16},{32,40},{40,32},{48,56},{56,48},{64,72... | collective-permute-start | bytes 3145736 | tf_op jit(solution)/shard_map/ppermute | solution.py:271
  64.0 3.5 %collective-permute-start.11 = (bf16[8,2,2,128,128]{4,3,2,1,0:T(8,128)(2,1)}, bf16[8,2,2,128,128]{4,3,2,1,0:T(8,128)(2,1)}, u32[]{:S(2)}, u32[]{:S(2)}) collective-permute-start(bf16[8,2,2,128,128]{4,3,2,1,0:T(8,128)(2,1)} %collective-permute-done.7.refs_1_), channel_id=1, source_target_pairs={{0,8},{8,0},{16,24},{24,16},{32,40},{40,32},{48,56},{56,48},{64,72... | collective-permute-start | bytes 3145736 | tf_op jit(solution)/shard_map/ppermute | solution.py:271
  67.5 0.1 pad_add_fusion.place
  67.6 7.1 %flip.1.basis = bf16[2048,2048]{1,0:T(8,128)(2,1)} custom-call(bf16[2048,2048]{1,0:T(8,128)(2,1)} %bitcast.23), custom_call_target="tpu_custom_call" | custom-call | bytes 16777216 | tf_op jit(solution)/shard_map/flip/pallas_call | solution.py:180
  74.7 3.0 %all-to-all-done.1.mine = bf16[16,2,128,128]{3,2,1,0:T(8,128)(2,1)} async-done(((bf16[16,2,128,128]{3,2,1,0:T(8,128)(2,1)}), bf16[16,2,128,128]{3,2,1,0:T(8,128)(2,1)}, u32[]{:S(2)}, u32[]{:S(2)}) %all-to-all-start.1) | async-done | bytes 1048608 | tf_op jit(solution)/shard_map/all_to_all | solution.py:272
  77.8 7.7 %rotate.1 = bf16[16,2,128,128]{3,2,1,0:T(8,128)(2,1)S(1)} custom-call(s32[3]{0:T(128)S(1)} %pad_add_fusion.place, bf16[16,2,128,128]{3,2,1,0:T(8,128)(2,1)} %all-to-all-done.1.mine, bf16[8,2,2,128,128]{4,3,2,1,0:T(8,128)(2,1)S(1)} %stack.17.refs_0_, bf16[8,2,2,128,128]{4,3,2,1,0:T(8,128)(2,1)} %collective-permute-done.7.refs_1_, ...), custom_call_target="tpu_custom_call" | custom-call | flops 4294967296 | bytes 33554432 | tf_op jit(solution)/shard_map/rotate/pallas_call | solution.py:140
  85.5 31.9 %all_to_all.15.back = bf16[16,2,128,128]{3,2,1,0:T(8,128)(2,1)S(1)} all-to-all(bf16[16,2,128,128]{3,2,1,0:T(8,128)(2,1)S(1)} %rotate.1), channel_id=1, replica_groups=mesh['dp'=2,'row'=16,'col'=8] {'row'}, dimensions={0} | all-to-all | bytes 2097152 | tf_op jit(solution)/shard_map/all_to_all | solution.py:275
  117.4 3.0 %finish.1 = (bf16[128,2048]{1,0:T(8,128)(2,1)}, f32[128,16,1,128]{3,2,1,0:T(1,128)}) custom-call(bf16[16,2,128,128]{3,2,1,0:T(8,128)(2,1)S(1)} %all_to_all.15.back, bf16[2048,2048]{1,0:T(8,128)(2,1)S(1)} %copy-done.1, f32[128,2048]{1,0:T(8,128)S(1)} %bitcast.17), custom_call_target="tpu_custom_call" | custom-call | tf_op jit(solution)/shard_map/finish/pallas_call | solution.py:217
  (16 shorter events, 0.1 us)
Async XLA Ops:
  0.6 10.1 %copy-start = (bf16[1,2048,128]{2,1,0:T(8,128)(2,1)S(1)}, bf16[1,2048,128]{2,1,0:T(8,128)(2,1)}, u32[]{:S(2)}) copy-start(bf16[1,2048,128]{2,1,0:T(8,128)(2,1)} %param.5) | copy-start | bytes 1572868
  3.1 26.6 %all-to-all-start = ((bf16[16,128,256]{2,1,0:T(8,128)(2,1)}), bf16[16,128,256]{2,1,0:T(8,128)(2,1)S(1)}, u32[]{:S(2)}, u32[]{:S(2)}) async-start(bf16[16,128,256]{2,1,0:T(8,128)(2,1)} %bitcast.5), calls=%async_computation | async-start | bytes 2097152 | tf_op jit(solution)/shard_map/all_to_all | solution.py:255
  10.8 7.6 %collective-permute-start.1 = (bf16[2,2,128,128]{3,2,1,0:T(8,128)(2,1)S(1)}, bf16[2,2,128,128]{3,2,1,0:T(8,128)(2,1)S(1)}, u32[]{:S(2)}, u32[]{:S(2)}) collective-permute-start(bf16[2,2,128,128]{3,2,1,0:T(8,128)(2,1)S(1)} %bitcast.19), channel_id=1, source_target_pairs={{16,0},{24,8},{32,16},{40,24},{48,32},{56,40},{64,48},{72,56},{80,... | collective-permute-start | bytes 393224 | tf_op jit(solution)/shard_map/ppermute | solution.py:252
  16.4 5.3 %collective-permute-start = (bf16[2,2,128,128]{3,2,1,0:T(8,128)(2,1)S(1)}, bf16[2,2,128,128]{3,2,1,0:T(8,128)(2,1)S(1)}, u32[]{:S(2)}, u32[]{:S(2)}) collective-permute-start(bf16[2,2,128,128]{3,2,1,0:T(8,128)(2,1)S(1)} %bitcast.20), channel_id=1, source_target_pairs={{0,16},{8,24},{16,32},{24,40},{32,48},{40,56},{48,64},{56,72},{64,... | collective-permute-start | bytes 393224 | tf_op jit(solution)/shard_map/ppermute | solution.py:252
  21.7 5.3 %collective-permute-start.2 = (bf16[2,2,128,128]{3,2,1,0:T(8,128)(2,1)S(1)}, bf16[2,2,128,128]{3,2,1,0:T(8,128)(2,1)S(1)}, u32[]{:S(2)}, u32[]{:S(2)}) collective-permute-start(bf16[2,2,128,128]{3,2,1,0:T(8,128)(2,1)S(1)} %collective-permute-done.refs_1_), channel_id=1, source_target_pairs={{0,16},{8,24},{16,32},{24,40},{32,48},{40,56},{48,64},{56,72},{64,... | collective-permute-start | bytes 393224 | tf_op jit(solution)/shard_map/ppermute | solution.py:262
  21.7 5.3 %collective-permute-start.3 = (bf16[2,2,128,128]{3,2,1,0:T(8,128)(2,1)S(1)}, bf16[2,2,128,128]{3,2,1,0:T(8,128)(2,1)S(1)}, u32[]{:S(2)}, u32[]{:S(2)}) collective-permute-start(bf16[2,2,128,128]{3,2,1,0:T(8,128)(2,1)S(1)} %collective-permute-done.1.refs_2_), channel_id=1, source_target_pairs={{16,0},{24,8},{32,16},{40,24},{48,32},{56,40},{64,48},{72,56},{80,... | collective-permute-start | bytes 393224 | tf_op jit(solution)/shard_map/ppermute | solution.py:262
  27.1 7.0 %collective-permute-start.6 = (bf16[2,2,128,128]{3,2,1,0:T(8,128)(2,1)S(1)}, bf16[2,2,128,128]{3,2,1,0:T(8,128)(2,1)S(1)}, u32[]{:S(2)}, u32[]{:S(2)}) collective-permute-start(bf16[2,2,128,128]{3,2,1,0:T(8,128)(2,1)S(1)} %collective-permute-done.2.refs_3_), channel_id=1, source_target_pairs={{0,32},{8,40},{16,48},{24,56},{32,64},{40,72},{48,80},{56,88},{64,... | collective-permute-start | bytes 393224 | tf_op jit(solution)/shard_map/ppermute | solution.py:264
  27.1 7.0 %collective-permute-start.4 = (bf16[2,2,128,128]{3,2,1,0:T(8,128)(2,1)S(1)}, bf16[2,2,128,128]{3,2,1,0:T(8,128)(2,1)S(1)}, u32[]{:S(2)}, u32[]{:S(2)}) collective-permute-start(bf16[2,2,128,128]{3,2,1,0:T(8,128)(2,1)S(1)} %collective-permute-done.2.refs_3_), channel_id=1, source_target_pairs={{0,16},{8,24},{16,32},{24,40},{32,48},{40,56},{48,64},{56,72},{64,... | collective-permute-start | bytes 393224 | tf_op jit(solution)/shard_map/ppermute | solution.py:262
  27.1 7.0 %collective-permute-start.5 = (bf16[2,2,128,128]{3,2,1,0:T(8,128)(2,1)S(1)}, bf16[2,2,128,128]{3,2,1,0:T(8,128)(2,1)}, u32[]{:S(2)}, u32[]{:S(2)}) collective-permute-start(bf16[2,2,128,128]{3,2,1,0:T(8,128)(2,1)S(1)} %collective-permute-done.3.refs_4_), channel_id=1, source_target_pairs={{16,0},{24,8},{32,16},{40,24},{48,32},{56,40},{64,48},{72,56},{80,... | collective-permute-start | bytes 393224 | tf_op jit(solution)/shard_map/ppermute | solution.py:262
  34.0 6.6 %copy-start.2 = (bf16[16,2,128,128]{3,2,1,0:T(8,128)(2,1)}, bf16[16,2,128,128]{3,2,1,0:T(8,128)(2,1)S(1)}, u32[]{:S(2)}) copy-start(bf16[16,2,128,128]{3,2,1,0:T(8,128)(2,1)S(1)} %half_rotate.1) | copy-start | bytes 3145732
  35.2 22.1 %collective-permute-start.9 = (bf16[8,2,2,128,128]{4,3,2,1,0:T(8,128)(2,1)S(1)}, bf16[8,2,2,128,128]{4,3,2,1,0:T(8,128)(2,1)}, u32[]{:S(2)}, u32[]{:S(2)}) collective-permute-start(bf16[8,2,2,128,128]{4,3,2,1,0:T(8,128)(2,1)S(1)} %stack.17.refs_0_), channel_id=1, source_target_pairs={{0,4},{1,5},{2,6},{3,7},{4,0},{5,1},{6,2},{7,3},{8,12},{9,13},{10,... | collective-permute-start | bytes 3145736 | tf_op jit(solution)/shard_map/ppermute | solution.py:270
  38.2 24.3 %collective-permute-start.8 = (bf16[8,2,2,128,128]{4,3,2,1,0:T(8,128)(2,1)S(1)}, bf16[8,2,2,128,128]{4,3,2,1,0:T(8,128)(2,1)}, u32[]{:S(2)}, u32[]{:S(2)}) collective-permute-start(bf16[8,2,2,128,128]{4,3,2,1,0:T(8,128)(2,1)S(1)} %stack.17.refs_0_), channel_id=1, source_target_pairs={{1,0},{2,1},{3,2},{0,3},{5,4},{6,5},{7,6},{4,7},{9,8},{10,9},{11,1... | collective-permute-start | bytes 3145736 | tf_op jit(solution)/shard_map/ppermute | solution.py:270
  40.6 23.4 %collective-permute-start.7 = (bf16[8,2,2,128,128]{4,3,2,1,0:T(8,128)(2,1)S(1)}, bf16[8,2,2,128,128]{4,3,2,1,0:T(8,128)(2,1)}, u32[]{:S(2)}, u32[]{:S(2)}) collective-permute-start(bf16[8,2,2,128,128]{4,3,2,1,0:T(8,128)(2,1)S(1)} %stack.17.refs_0_), channel_id=1, source_target_pairs={{0,1},{1,2},{2,3},{3,0},{4,5},{5,6},{6,7},{7,4},{8,9},{9,10},{10,1... | collective-permute-start | bytes 3145736 | tf_op jit(solution)/shard_map/ppermute | solution.py:270
  40.6 37.1 %all-to-all-start.1 = ((bf16[16,2,128,128]{3,2,1,0:T(8,128)(2,1)}), bf16[16,2,128,128]{3,2,1,0:T(8,128)(2,1)}, u32[]{:S(2)}, u32[]{:S(2)}) async-start(bf16[16,2,128,128]{3,2,1,0:T(8,128)(2,1)} %copy-done.2), calls=%async_computation.1 | async-start | bytes 2097152 | tf_op jit(solution)/shard_map/all_to_all | solution.py:272
  49.7 28.1 %collective-permute-start.10 = (bf16[8,2,2,128,128]{4,3,2,1,0:T(8,128)(2,1)S(1)}, bf16[8,2,2,128,128]{4,3,2,1,0:T(8,128)(2,1)}, u32[]{:S(2)}, u32[]{:S(2)}) collective-permute-start(bf16[8,2,2,128,128]{4,3,2,1,0:T(8,128)(2,1)S(1)} %stack.17.refs_0_), channel_id=1, source_target_pairs={{0,8},{8,0},{16,24},{24,16},{32,40},{40,32},{48,56},{56,48},{64,72... | collective-permute-start | bytes 3145736 | tf_op jit(solution)/shard_map/ppermute | solution.py:271
  57.3 20.5 %collective-permute-start.13 = (bf16[8,2,2,128,128]{4,3,2,1,0:T(8,128)(2,1)}, bf16[8,2,2,128,128]{4,3,2,1,0:T(8,128)(2,1)}, u32[]{:S(2)}, u32[]{:S(2)}) collective-permute-start(bf16[8,2,2,128,128]{4,3,2,1,0:T(8,128)(2,1)} %collective-permute-done.9.refs_3_), channel_id=1, source_target_pairs={{0,8},{8,0},{16,24},{24,16},{32,40},{40,32},{48,56},{56,48},{64,72... | collective-permute-start | bytes 3145736 | tf_op jit(solution)/shard_map/ppermute | solution.py:271
  62.5 15.3 %collective-permute-start.12 = (bf16[8,2,2,128,128]{4,3,2,1,0:T(8,128)(2,1)}, bf16[8,2,2,128,128]{4,3,2,1,0:T(8,128)(2,1)}, u32[]{:S(2)}, u32[]{:S(2)}) collective-permute-start(bf16[8,2,2,128,128]{4,3,2,1,0:T(8,128)(2,1)} %collective-permute-done.8.refs_2_), channel_id=1, source_target_pairs={{0,8},{8,0},{16,24},{24,16},{32,40},{40,32},{48,56},{56,48},{64,72... | collective-permute-start | bytes 3145736 | tf_op jit(solution)/shard_map/ppermute | solution.py:271
  64.0 13.8 %collective-permute-start.11 = (bf16[8,2,2,128,128]{4,3,2,1,0:T(8,128)(2,1)}, bf16[8,2,2,128,128]{4,3,2,1,0:T(8,128)(2,1)}, u32[]{:S(2)}, u32[]{:S(2)}) collective-permute-start(bf16[8,2,2,128,128]{4,3,2,1,0:T(8,128)(2,1)} %collective-permute-done.7.refs_1_), channel_id=1, source_target_pairs={{0,8},{8,0},{16,24},{24,16},{32,40},{40,32},{48,56},{56,48},{64,72... | collective-permute-start | bytes 3145736 | tf_op jit(solution)/shard_map/ppermute | solution.py:271
  77.8 39.6 %copy-start.1 = (bf16[2048,2048]{1,0:T(8,128)(2,1)S(1)}, bf16[2048,2048]{1,0:T(8,128)(2,1)}, u32[]{:S(2)}) copy-start(bf16[2048,2048]{1,0:T(8,128)(2,1)} %flip.1.basis) | copy-start | bytes 25165828
